TPU v7x, 32 devices: a whole 2x2x4 slice. The times are simulated.
32 devices in a mesh: seq: 16 (over z, x, core), fsdp: 2 (over y).
Axes of the slice: x: 2, y: 2, z: 4, core: 2. Of those that a mesh axis runs over, the one named last changes fastest.
Arguments:
- hidden_in: bfloat16 [4, 3072, 1024], P('fsdp', 'seq'), may hold values from -6 to 6
- cotangent: bfloat16 [4, 3072, 1024], P('fsdp', 'seq'), may hold values from -6 to 6
- norm_gain: float32 [1024], replicated, may hold values from 0.5 to 1.5
- in_weight: bfloat16 [1024, 4384], P('fsdp'), may hold values from -0.1875 to 0.1875
- conv_weight: float32 [4, 2304], replicated, may hold values from -3 to 3
- conv_bias: float32 [2304], replicated, may hold values from -0.5 to 0.5
- dt_bias: float32 [32], replicated, may hold values from -6.5 to -2.5
- a_log: float32 [32], replicated, may hold values from 0 to 2.75
- skip_gain: float32 [32], replicated, may hold values from 0.5 to 1.5
- gate_gain: float32 [2048], replicated, may hold values from 0.5 to 1.5
- out_weight: bfloat16 [2048, 1024], P('fsdp'), may hold values from -0.125 to 0.125
Outputs:
- hidden_out: bfloat16 [4, 3072, 1024], P('fsdp', 'seq')
- grad_hidden: float32 [4, 3072, 1024], P('fsdp', 'seq')
- grad_norm_gain: float32 [1024], replicated
- grad_in_weight: float32 [1024, 4384], P('fsdp')
- grad_conv_weight: float32 [4, 2304], replicated
- grad_conv_bias: float32 [2304], replicated
- grad_dt_bias: float32 [32], replicated
- grad_a_log: float32 [32], replicated
- grad_skip_gain: float32 [32], replicated
- grad_gate_gain: float32 [2048], replicated
- grad_out_weight: float32 [2048, 1024], P('fsdp')
All inputs are finite; a program needn't handle non-finite values.
Results may differ from a plain program's by a relative error of at most 0.004.
The roundings to bfloat16 on the way count: a program that leaves them out, or rounds other values in their place, can miss the bound.
Values may be sent and summed in bfloat16 or wider, within the bound.
No kernel may reach another device: no remote copies, remote signals or barrier semaphores. Data moves between devices by JAX's collectives and lax.ppermute only.
A program may use at most 320 MiB of HBM per device.

v0:
```python
import jax
import jax.numpy as jnp
from jax import lax
from jax.sharding import PartitionSpec as P

HEADDIM = 64
STATE = 128
CONV = 4
SPAN = 256


norm_eps = 1e-05


def ssd_span(carried, pieces):
    span_values, span_steps, span_decay, span_write, span_read = pieces
    cumulative = jnp.cumsum(span_decay, axis=0)
    products = jnp.dot(span_read, span_write.T, precision=lax.Precision.HIGHEST)
    differences = cumulative.T[:, :, None] - cumulative.T[:, None, :]
    row_index = lax.broadcasted_iota(jnp.int32, differences.shape, 1)
    col_index = lax.broadcasted_iota(jnp.int32, differences.shape, 2)
    decays = jnp.exp(jnp.where(row_index >= col_index, differences, -jnp.inf))
    weights = products[None, :, :] * decays * span_steps.T[:, None, :]
    within = jnp.einsum("hij,jhp->ihp", weights, span_values, precision=lax.Precision.HIGHEST)
    from_state = jnp.einsum("in,hnp->ihp", span_read, carried, precision=lax.Precision.HIGHEST)
    from_state = from_state * jnp.exp(cumulative)[:, :, None]
    to_end = jnp.exp(cumulative[-1][None, :] - cumulative) * span_steps
    new_state = jnp.exp(cumulative[-1])[:, None, None] * carried + jnp.einsum(
        "jn,jhp->hnp", span_write, span_values * to_end[:, :, None], precision=lax.Precision.HIGHEST
    )
    return (new_state, within + from_state)


def ssd(values, step_size, log_decay, write_side, read_side):
    length, head_count, head_dim = values.shape
    span_count = length // SPAN
    pieces = (
        values.reshape(span_count, SPAN, head_count, head_dim),
        step_size.reshape(span_count, SPAN, head_count),
        log_decay.reshape(span_count, SPAN, head_count),
        write_side.reshape(span_count, SPAN, write_side.shape[1]),
        read_side.reshape(span_count, SPAN, read_side.shape[1]),
    )
    initial = jnp.zeros((head_count, write_side.shape[1], head_dim), jnp.float32)
    _, outputs = lax.scan(jax.checkpoint(ssd_span), initial, pieces)
    return outputs.reshape(length, head_count, head_dim)


def mixer(x_part, dt_raw, shared_part, conv_w, conv_b, dt_shift, log_rate, skip_w):
    length = x_part.shape[0]
    head_count = dt_raw.shape[1]
    head_width = head_count * HEADDIM
    joined = jnp.concatenate([x_part, shared_part], axis=1)
    padded = jnp.pad(joined, ((CONV - 1, 0), (0, 0)))
    convolved = conv_b[None, :] + jnp.zeros_like(joined)
    for offset in range(CONV):
        convolved = convolved + conv_w[offset][None, :] * padded[offset : offset + length]
    activated = jax.nn.silu(convolved)
    values = activated[:, :head_width].reshape(length, head_count, HEADDIM)
    write_side = activated[:, head_width : head_width + STATE]
    read_side = activated[:, head_width + STATE :]
    step_size = jax.nn.softplus(dt_raw + dt_shift[None, :])
    log_decay = -step_size * jnp.exp(log_rate)[None, :]
    scanned = ssd(values, step_size, log_decay, write_side, read_side)
    return (scanned + skip_w[None, :, None] * values).reshape(length, head_width)


def prenorm(rows_in, gain):
    return (
        rows_in * lax.rsqrt(jnp.mean(rows_in * rows_in, axis=-1, keepdims=True) + norm_eps) * gain
    )


def gate_norm(mixed_in, gate_in, gain):
    gated = mixed_in * jax.nn.silu(gate_in)
    return gated * lax.rsqrt(jnp.mean(gated * gated, axis=-1, keepdims=True) + norm_eps) * gain


def per_device(
    hidden_in,
    cotangent,
    norm_gain,
    in_weight,
    conv_weight,
    conv_bias,
    dt_bias,
    a_log,
    skip_gain,
    gate_gain,
    out_weight,
):
    seq_count = lax.axis_size("seq")
    seq_slot = lax.axis_index("seq")
    group_seqs, local_len, width = hidden_in.shape
    token_rows = group_seqs * local_len
    total_heads = dt_bias.shape[0]
    head_count = total_heads // seq_count
    head_width = head_count * HEADDIM
    inner_width = total_heads * HEADDIM
    shared_width = 2 * STATE
    full_len = local_len * seq_count
    residual = hidden_in.reshape(token_rows, width).astype(jnp.float32)
    scaled, norm_back = jax.vjp(prenorm, residual, norm_gain)
    scaled_low = scaled.astype(jnp.bfloat16)
    in_full, out_full = (
        lax.all_gather(in_weight, "fsdp", axis=0, tiled=True),
        lax.all_gather(out_weight, "fsdp", axis=0, tiled=True),
    )
    projected = jnp.dot(scaled_low, in_full, preferred_element_type=jnp.float32).astype(
        jnp.bfloat16
    )
    gate_part = projected[:, :inner_width]
    x_part = projected[:, inner_width : 2 * inner_width].reshape(
        group_seqs, local_len, seq_count, head_width
    )
    shared_part = projected[:, 2 * inner_width : 2 * inner_width + shared_width].reshape(
        group_seqs, local_len, shared_width
    )
    dt_part = projected[:, 2 * inner_width + shared_width :].reshape(
        group_seqs, local_len, seq_count, head_count
    )
    x_heads, dt_heads = (
        lax.all_to_all(x_part, "seq", split_axis=2, concat_axis=1, tiled=True),
        lax.all_to_all(dt_part, "seq", split_axis=2, concat_axis=1, tiled=True),
    )
    shared_heads = lax.all_gather(shared_part, "seq", axis=1, tiled=True)
    x_heads = x_heads.reshape(group_seqs, full_len, head_width).astype(jnp.float32)
    dt_heads = dt_heads.reshape(group_seqs, full_len, head_count).astype(jnp.float32)
    shared_heads = shared_heads.astype(jnp.float32)
    conv_local = jnp.concatenate(
        [
            lax.dynamic_slice_in_dim(conv_weight, seq_slot * head_width, head_width, 1),
            conv_weight[:, inner_width:],
        ],
        axis=1,
    )
    bias_local = jnp.concatenate(
        [
            lax.dynamic_slice_in_dim(conv_bias, seq_slot * head_width, head_width, 0),
            conv_bias[inner_width:],
        ],
        axis=0,
    )
    shift_local = lax.dynamic_slice_in_dim(dt_bias, seq_slot * head_count, head_count, 0)
    rate_local = lax.dynamic_slice_in_dim(a_log, seq_slot * head_count, head_count, 0)
    skip_local = lax.dynamic_slice_in_dim(skip_gain, seq_slot * head_count, head_count, 0)
    batched = jax.vmap(mixer, in_axes=(0, 0, 0, None, None, None, None, None))
    mixed_heads, mixer_back = jax.vjp(
        batched,
        x_heads,
        dt_heads,
        shared_heads,
        conv_local,
        bias_local,
        shift_local,
        rate_local,
        skip_local,
    )
    mixed_send = mixed_heads.astype(jnp.bfloat16).reshape(group_seqs, full_len, 1, head_width)
    mixed_tokens = lax.all_to_all(
        mixed_send, "seq", split_axis=1, concat_axis=2, tiled=True
    ).reshape(token_rows, inner_width)
    normed, gate_back = jax.vjp(
        gate_norm, mixed_tokens.astype(jnp.float32), gate_part.astype(jnp.float32), gate_gain
    )
    normed_low = normed.astype(jnp.bfloat16)
    result = residual + jnp.dot(normed_low, out_full, preferred_element_type=jnp.float32)
    hidden_out = result.astype(jnp.bfloat16).reshape(hidden_in.shape)
    grad_rows = cotangent.reshape(token_rows, width)
    in_back, out_back = (
        lax.all_gather(in_weight, "fsdp", axis=0, tiled=True),
        lax.all_gather(out_weight, "fsdp", axis=0, tiled=True),
    )
    out_weight_part = lax.dot_general(
        normed_low, grad_rows, (((0,), (0,)), ((), ())), preferred_element_type=jnp.float32
    )
    grad_normed = lax.dot_general(
        grad_rows, out_back, (((1,), (1,)), ((), ())), preferred_element_type=jnp.float32
    )
    grad_mixed, grad_gate, gate_gain_part = gate_back(grad_normed)
    grad_send = grad_mixed.astype(jnp.bfloat16).reshape(
        group_seqs, local_len, seq_count, head_width
    )
    grad_heads = lax.all_to_all(grad_send, "seq", split_axis=2, concat_axis=1, tiled=True)
    grad_heads = grad_heads.reshape(group_seqs, full_len, head_width).astype(jnp.float32)
    grad_x, grad_dt, grad_shared, grad_conv, grad_bias, grad_shift, grad_rate, grad_skip = (
        mixer_back(grad_heads)
    )
    back_x = grad_x.astype(jnp.bfloat16).reshape(group_seqs, full_len, 1, head_width)
    back_dt = grad_dt.astype(jnp.bfloat16).reshape(group_seqs, full_len, 1, head_count)
    token_x, token_dt = (
        lax.all_to_all(back_x, "seq", split_axis=1, concat_axis=2, tiled=True),
        lax.all_to_all(back_dt, "seq", split_axis=1, concat_axis=2, tiled=True),
    )
    token_shared = lax.psum_scatter(
        grad_shared.astype(jnp.bfloat16), "seq", scatter_dimension=1, tiled=True
    )
    grad_projected = jnp.concatenate(
        [
            grad_gate.astype(jnp.bfloat16),
            token_x.reshape(token_rows, inner_width),
            token_shared.reshape(token_rows, shared_width),
            token_dt.reshape(token_rows, total_heads),
        ],
        axis=1,
    )
    in_weight_part = lax.dot_general(
        scaled_low, grad_projected, (((0,), (0,)), ((), ())), preferred_element_type=jnp.float32
    )
    grad_scaled = lax.dot_general(
        grad_projected, in_back, (((1,), (1,)), ((), ())), preferred_element_type=jnp.float32
    )
    grad_resid, norm_gain_part = norm_back(grad_scaled)
    grad_hidden = (grad_rows.astype(jnp.float32) + grad_resid).reshape(hidden_in.shape)
    in_shard, out_shard = (
        lax.psum_scatter(in_weight_part, "fsdp", scatter_dimension=0, tiled=True),
        lax.psum_scatter(out_weight_part, "fsdp", scatter_dimension=0, tiled=True),
    )
    in_total, out_total = lax.psum((in_shard, out_shard), "seq")
    conv_full = lax.dynamic_update_slice_in_dim(
        jnp.zeros((CONV, inner_width), jnp.float32),
        grad_conv[:, :head_width],
        seq_slot * head_width,
        1,
    )
    conv_full = jnp.concatenate([conv_full, grad_conv[:, head_width:]], axis=1)
    bias_full = lax.dynamic_update_slice_in_dim(
        jnp.zeros((inner_width,), jnp.float32), grad_bias[:head_width], seq_slot * head_width, 0
    )
    bias_full = jnp.concatenate([bias_full, grad_bias[head_width:]], axis=0)
    head_zeros = jnp.zeros((total_heads,), jnp.float32)
    shift_full = lax.dynamic_update_slice_in_dim(head_zeros, grad_shift, seq_slot * head_count, 0)
    rate_full = lax.dynamic_update_slice_in_dim(head_zeros, grad_rate, seq_slot * head_count, 0)
    skip_full = lax.dynamic_update_slice_in_dim(head_zeros, grad_skip, seq_slot * head_count, 0)
    norm_sum, conv_sum, bias_sum, shift_sum, rate_sum, skip_sum, gate_sum = lax.psum(
        (norm_gain_part, conv_full, bias_full, shift_full, rate_full, skip_full, gate_gain_part),
        ("seq", "fsdp"),
    )
    return (
        hidden_out,
        grad_hidden,
        norm_sum,
        in_total,
        conv_sum,
        bias_sum,
        shift_sum,
        rate_sum,
        skip_sum,
        gate_sum,
        out_total,
    )


def solution(mesh):
    placed = (
        P("fsdp", "seq", None),
        P("fsdp", "seq", None),
        P(),
        P("fsdp", None),
        P(),
        P(),
        P(),
        P(),
        P(),
        P(),
        P("fsdp", None),
    )
    return jax.shard_map(
        per_device,
        mesh=mesh,
        in_specs=placed,
        out_specs=(
            P("fsdp", "seq", None),
            P("fsdp", "seq", None),
            P(),
            P("fsdp", None),
            P(),
            P(),
            P(),
            P(),
            P(),
            P(),
            P("fsdp", None),
        ),
        check_vma=False,
    )
```

profile of v0, /device:TPU:0, one launch (start us, length us, event | category | flops | bytes accessed | tf_op | source)
XLA Modules:
  0.0 1527.3 jit_solution(9769375290916082267)
XLA Ops:
  10.4 114.9 %all-gather.4.cloned.1.call-done = bf16[1024,4384]{0,1:T(8,128)(2,1)} async-done(((bf16[512,4384]{0,1:T(8,128)(2,1)}), bf16[1024,4384]{0,1:T(8,128)(2,1)}) %all-gather.4.cloned.1.call-update) | async-done | bytes 8978448 | tf_op jit(solution)/shard_map/all_gather | solution.py:106
  125.3 8.7 convolution_convert_fusion
  137.5 5.6 all-to-all-start
  144.4 5.1 reshape.590
  149.5 3.5 copy.250
  153.1 6.1 all-to-all-start.1
  162.0 41.9 %all-to-all-done.1 = bf16[2,192,16,128]{3,1,0,2:T(8,128)(2,1)S(1)} async-done(((bf16[2,192,16,128]{3,1,0,2:T(8,128)(2,1)}), bf16[2,192,16,128]{3,1,0,2:T(8,128)(2,1)S(1)}, u32[]{:S(2)}, u32[]{:S(2)}) %all-to-all-start.1) | async-done | bytes 1572896 | tf_op jit(solution)/shard_map/all_to_all | solution.py:123
  207.1 8.5 fusion.75
  215.7 3.9 fusion.121
  226.9 5.9 copy.255
  238.5 120.8 %while.41 = (s32[]{:T(128)}, f32[2,2,128,64]{2,3,1,0:T(8,128)S(1)}, f32[12,2,256,2,64]{2,4,3,1,0:T(8,128)}, f32[12,2,2,128,64]{3,4,2,1,0:T(8,128)}, f32[12,2,256...) while((s32[]{:T(128)}, f32[2,2,128,64]{2,3,1,0:T(8,128)S(1)}, ...), condition=%wide.region_4.5_spmd.clone, body=%wide.region_1.4_spmd.clone.sunk | while | flops 605456384 | bytes 4415911 | solution.py:45
  359.3 9.6 copy.302
  368.9 7.1 reshape.591
  379.2 13.4 copy.261
  392.6 45.6 %all_to_all.66 = bf16[2,3072,1,128]{3,0,2,1:T(2,128)(2,1)S(1)} all-to-all(bf16[2,3072,1,128]{3,0,2,1:T(2,128)(2,1)S(1)} %copy.261), channel_id=1, replica_groups=mesh['seq'=16,'fsdp'=2] {'seq'}, dimensions={1} | all-to-all | bytes 3145728 | tf_op jit(solution)/shard_map/all_to_all | solution.py:160
  438.8 4.3 copy.309
  443.1 6.0 reshape.595
  452.6 6.9 multiply_reduce_fusion.9
  459.5 4.4 fusion.82
  463.9 5.1 reshape.592
  469.0 3.5 copy.268
  472.6 5.1 all-to-all-start.3
  477.7 32.0 %all-to-all-done.3 = bf16[2,192,16,128]{3,1,0,2:T(8,128)(2,1)} async-done(((bf16[2,192,16,128]{3,1,0,2:T(8,128)(2,1)}), bf16[2,192,16,128]{3,1,0,2:T(8,128)(2,1)}, u32[]{:S(2)}, u32[]{:S(2)}) %all-to-all-start.3) | async-done | bytes 1572896 | tf_op jit(solution)/shard_map/all_to_all | solution.py:184
  509.7 3.9 bitcast_convert_fusion
  513.6 3.5 copy.270
  517.0 5.8 reshape.568
  528.9 274.3 %while.42 = (s32[]{:T(128)}, f32[2,2,128,64]{2,3,1,0:T(8,128)S(1)}, f32[12,2,256,2,64]{2,4,3,1,0:T(8,128)}, f32[12,2,256,2]{2,0,3,1:T(8,128)S(1)}, f32[12,2,256,...) while((s32[]{:T(128)}, f32[2,2,128,64]{2,3,1,0:T(8,128)S(1)}, ...), condition=%wide.region_20.21_spmd.clone, body=%wide.region_7.20_spmd.clone.sunk | while | flops 1515563008 | bytes 14648275 | solution.py:45
  541.8 5.1 reduce-window.74
  564.7 5.1 reduce-window.74
  587.5 5.1 reduce-window.74
  610.4 5.1 reduce-window.74
  633.2 5.1 reduce-window.74
  656.1 5.1 reduce-window.74
  678.9 5.1 reduce-window.74
  701.8 5.1 reduce-window.74
  724.6 5.1 reduce-window.74
  747.5 5.1 reduce-window.74
  770.3 5.1 reduce-window.74
  793.2 5.1 reduce-window.74
  803.2 9.4 copy.305
  812.6 7.5 reshape.593
  820.1 4.3 multiply_reduce_fusion.10
  826.2 19.4 %multiply_reduce_fusion.7 = (f32[384]{0:T(512)}, f32[384]{0:T(512)}, f32[384]{0:T(512)}, f32[384]{0:T(512)}, f32[384]{0:T(512)}, /*index=5*/f32[2,3072,384]{2,1,0:T(8,128)}) fusion(f32[2,3072,384]{2,1,0:T(8,128)} %copy-done.2, bf16[2,3072,256]{2,1,0:T(8,128)(2,1)S(1)} %copy-done.10, bf16[2,3072,128]{2,1,0:T(8,128)(2,1)S(1)} %bitcast.423, ...), kind=kLoop, calls=%fused_computation.123 | loop fusion | flops 56621184 | bytes 42475008 | tf_op jit(solution)/shard_map/transpose(jvp(vmap()))/reduce_sum | solution.py:57
  845.6 10.7 broadcast_multiply_fusion
  856.3 3.7 copy-done
  862.7 6.9 fusion.76
  871.5 6.9 fusion.117
  883.1 4.9 reshape.605
  888.0 9.1 all-to-all-start.5
  897.1 5.8 fusion.85
  902.9 13.8 copy.281
  916.7 6.1 all-to-all-start.4
  922.8 4.5 reshape.606
  930.8 30.3 %all-to-all-done.4 = bf16[2,3072,1,128]{3,0,2,1:T(2,128)(2,1)} async-done(((bf16[2,3072,1,128]{3,0,2,1:T(2,128)(2,1)}), bf16[2,3072,1,128]{3,0,2,1:T(2,128)(2,1)}, u32[]{:S(2)}, u32[]{:S(2)}) %all-to-all-start.4) | async-done | bytes 1572896 | tf_op jit(solution)/shard_map/all_to_all | solution.py:192
  963.9 6.2 copy.306
  970.0 5.4 reshape.594
  976.5 13.2 fusion.94
  989.8 67.9 %reduce-scatter.8.cloned.1.call-done = f32[1024,1024]{1,0:T(8,128)} async-done(((f32[2048,1024]{1,0:T(8,128)}), f32[1024,1024]{1,0:T(8,128)}) %reduce-scatter.8.cloned.1.call-update) | async-done | bytes 4194320 | tf_op jit(solution)/shard_map/reduce_scatter | solution.py:217
  1057.6 204.1 %reduce-scatter.6.cloned.1.call-done = f32[512,4384]{0,1:T(8,128)} async-done(((f32[1024,4384]{0,1:T(8,128)}), f32[512,4384]{0,1:T(8,128)}) %reduce-scatter.6.cloned.1.call-update) | async-done | bytes 8978448 | tf_op jit(solution)/shard_map/reduce_scatter | solution.py:216
  1261.8 5.2 fusion.91
  1270.7 9.6 fusion.89
  1280.3 42.2 %all-reduce.14 = (f32[1024]{0:T(1024)}, f32[4,2304]{1,0:T(4,128)}, f32[2304]{0:T(1024)}, f32[32]{0:T(128)}, f32[32]{0:T(128)}, /*index=5*/f32[32]{0:T(128)}, f32[2048]{0:T(1024)}) all-reduce(f32[1024]{0:T(1024)S(1)} %get-tuple-element.636, f32[4,2304]{1,0:T(4,128)S(1)} %pad_maximum_fusion.3, ...), channel_id=1, replica_groups=mesh['seq'=16,'fsdp'=2] {'seq','fsdp'}, use_global_device_ids=true, to_apply=%region_24.25 | all-reduce | flops 14688 | bytes 117504 | tf_op jit(solution)/shard_map/psum | solution.py:235
  1324.2 185.7 %all-reduce.18.cloned.1.call-done = (f32[512,4384]{0,1:T(8,128)}, f32[1024,1024]{1,0:T(8,128)}) async-done(((f32[512,4384]{0,1:T(8,128)}, f32[1024,1024]{1,0:T(8,128)}), (f32[512,4384]{0,1:T(8,128)}, f32[1024,1024]{1,0:T(8,128)})) %all-reduce.18.cloned.1.call-update) | async-done | bytes 13172752 | tf_op jit(solution)/shard_map/psum | solution.py:219
  1509.9 8.4 copy.413
  (925 shorter events, 398.2 us)
Async XLA Ops:
  7.2 118.1 %all-gather.4.cloned.1.call-start = ((), (), s32[]{:S(2)}) async-start(), calls=%async_computation.9 | async-start | bytes 13467648 | tf_op jit(solution)/shard_map/all_gather | solution.py:106
  7.9 196.1 %all-gather.6.cloned.1.call-start = ((), (), s32[]{:S(2)}) async-start(), calls=%async_computation.10 | async-start | bytes 3342336 | tf_op jit(solution)/shard_map/all_gather | solution.py:126
  134.0 9.1 copy-start.16
  137.5 15.6 %all-to-all-start = ((bf16[2,192,16,2]{1,3,0,2:T(2,128)(2,1)}), bf16[2,192,16,2]{1,3,0,2:T(2,128)(2,1)S(1)}, u32[]{:S(2)}, u32[]{:S(2)}) async-start(bf16[2,192,16,2]{1,3,0,2:T(2,128)(2,1)} %copy.247), calls=%async_computation | async-start | bytes 65536 | tf_op jit(solution)/shard_map/all_to_all | solution.py:124
  153.1 7.0 copy-start.52
  153.1 7.1 copy-start.56
  153.1 7.1 copy-start.57
  153.1 7.9 copy-start.41
  153.1 7.9 slice-start
  153.1 7.9 copy-start.55
  153.1 8.0 slice-start.1
  153.1 50.7 %all-to-all-start.1 = ((bf16[2,192,16,128]{3,1,0,2:T(8,128)(2,1)}), bf16[2,192,16,128]{3,1,0,2:T(8,128)(2,1)S(1)}, u32[]{:S(2)}, u32[]{:S(2)}) async-start(bf16[2,192,16,128]{3,1,0,2:T(8,128)(2,1)} %copy.250), calls=%async_computation.1 | async-start | bytes 3145728 | tf_op jit(solution)/shard_map/all_to_all | solution.py:123
  159.3 293.3 %all-gather.8.cloned.1.call-start = ((), (), s32[]{:S(2)}) async-start(), calls=%async_computation.11 | async-start | bytes 6291456 | tf_op jit(solution)/shard_map/all_gather | solution.py:107
  161.0 46.1 %copy-start.29 = (f32[384]{0:T(512)}, f32[384]{0:T(512)S(1)}, u32[]{:S(2)}) copy-start(f32[384]{0:T(512)S(1)} %get-tuple-element.641) | copy-start | bytes 4612
  161.0 46.1 %copy-start.31 = (f32[384]{0:T(512)}, f32[384]{0:T(512)S(1)}, u32[]{:S(2)}) copy-start(f32[384]{0:T(512)S(1)} %get-tuple-element.642) | copy-start | bytes 4612
  161.0 46.1 %copy-start.33 = (f32[384]{0:T(512)}, f32[384]{0:T(512)S(1)}, u32[]{:S(2)}) copy-start(f32[384]{0:T(512)S(1)} %get-tuple-element.643) | copy-start | bytes 4612
  161.1 45.9 %copy-start.50 = (f32[2]{0:T(128)}, f32[2]{0:T(128)S(1)}, u32[]{:S(2)}) copy-start(f32[2]{0:T(128)S(1)} %dynamic-slice_exponential_fusion) | copy-start | bytes 28
  207.1 8.6 copy-start.2
  359.3 9.6 copy-start.7
  368.9 7.1 copy-start.53
  472.6 37.1 %all-to-all-start.3 = ((bf16[2,192,16,128]{3,1,0,2:T(8,128)(2,1)}), bf16[2,192,16,128]{3,1,0,2:T(8,128)(2,1)}, u32[]{:S(2)}, u32[]{:S(2)}) async-start(bf16[2,192,16,128]{3,1,0,2:T(8,128)(2,1)} %copy.268), calls=%async_computation.3 | async-start | bytes 3145728 | tf_op jit(solution)/shard_map/all_to_all | solution.py:184
  477.7 497.8 %reduce-scatter.4.cloned.1.call-start = ((), (), s32[]{:S(2)}) async-start(), calls=%async_computation.12 | async-start | bytes 3342336 | tf_op jit(solution)/shard_map/reduce_scatter | solution.py:195
  528.9 9.0 copy-start.25
  539.9 11.9 copy-start.26
  551.8 9.0 copy-start.25
  562.8 11.8 copy-start.26
  574.6 9.0 copy-start.25
  585.6 11.9 copy-start.26
  597.5 9.0 copy-start.25
  608.5 11.9 copy-start.26
  620.4 9.0 copy-start.25
  631.4 11.8 copy-start.26
  643.2 9.0 copy-start.25
  654.2 11.9 copy-start.26
  666.0 9.0 copy-start.25
  677.0 11.9 copy-start.26
  688.9 9.0 copy-start.25
  699.9 11.8 copy-start.26
  711.8 9.0 copy-start.25
  722.7 11.9 copy-start.26
  734.6 9.0 copy-start.25
  745.6 11.8 copy-start.26
  757.5 9.0 copy-start.25
  768.5 11.8 copy-start.26
  780.3 9.0 copy-start.25
  791.3 11.9 copy-start.26
  812.6 7.5 copy-start.15
  812.6 7.5 copy-start.54
  826.2 19.5 %copy-start.30 = (f32[384]{0:T(512)S(1)}, f32[384]{0:T(512)}, u32[]{:S(2)}) copy-start(f32[384]{0:T(512)} %copy-done.29) | copy-start | bytes 4612
  826.2 19.5 %copy-start.32 = (f32[384]{0:T(512)S(1)}, f32[384]{0:T(512)}, u32[]{:S(2)}) copy-start(f32[384]{0:T(512)} %copy-done.31) | copy-start | bytes 4612
  826.2 19.5 %copy-start.34 = (f32[384]{0:T(512)S(1)}, f32[384]{0:T(512)}, u32[]{:S(2)}) copy-start(f32[384]{0:T(512)} %copy-done.33) | copy-start | bytes 4612
  869.6 188.0 %reduce-scatter.8.cloned.1.call-start = ((), (), s32[]{:S(2)}) async-start(), calls=%async_computation.14 | async-start | bytes 12582912 | tf_op jit(solution)/shard_map/reduce_scatter | solution.py:217
  888.0 28.7 %all-to-all-start.5 = ((bf16[16,2,384]{2,1,0:T(2,128)(2,1)}), bf16[16,2,384]{2,1,0:T(2,128)(2,1)S(1)}, u32[]{:S(2)}, u32[]{:S(2)}) async-start(bf16[16,2,384]{2,1,0:T(2,128)(2,1)} %reshape.605), calls=%async_computation.6 | async-start | bytes 49152 | tf_op jit(solution)/shard_map/all_to_all | solution.py:193
  916.7 44.4 %all-to-all-start.4 = ((bf16[2,3072,1,128]{3,0,2,1:T(2,128)(2,1)}), bf16[2,3072,1,128]{3,0,2,1:T(2,128)(2,1)}, u32[]{:S(2)}, u32[]{:S(2)}) async-start(bf16[2,3072,1,128]{3,0,2,1:T(2,128)(2,1)} %copy.281), calls=%async_computation.4 | async-start | bytes 3145728 | tf_op jit(solution)/shard_map/all_to_all | solution.py:192
  922.8 339.0 %reduce-scatter.6.cloned.1.call-start = ((), (), s32[]{:S(2)}) async-start(), calls=%async_computation.13 | async-start | bytes 26935296 | tf_op jit(solution)/shard_map/reduce_scatter | solution.py:216
  930.8 45.7 %copy-start.28 = (bf16[384,32]{0,1:T(8,128)(2,1)}, bf16[384,32]{0,1:T(8,128)(2,1)S(1)}, u32[]{:S(2)}) copy-start(bf16[384,32]{0,1:T(8,128)(2,1)S(1)} %reshape.560) | copy-start | bytes 73732
  989.7 520.1 %all-reduce.18.cloned.1.call-start = ((), (), s32[]{:S(2)}) async-start(), calls=%async_computation.15 | async-start | bytes 26345472 | tf_op jit(solution)/shard_map/psum | solution.py:219
  1261.8 8.8 copy-start.36
  1270.6 9.7 copy-start.47
  1270.6 51.9 %copy-start.38 = (f32[384]{0:T(512)S(1)}, f32[384]{0:T(512)}, u32[]{:S(2)}) copy-start(f32[384]{0:T(512)} %copy-done.37) | copy-start | bytes 4612
  1270.6 51.9 %copy-start.18 = (bf16[2,192,1024]{2,1,0:T(8,128)(2,1)S(1)}, bf16[2,192,1024]{2,1,0:T(8,128)(2,1)}, u32[]{:S(2)}) copy-start(bf16[2,192,1024]{2,1,0:T(8,128)(2,1)} %param.15) | copy-start | bytes 2359300
  1270.6 51.9 %copy-start.20 = (bf16[2,192,1024]{2,1,0:T(8,128)(2,1)S(1)}, bf16[2,192,1024]{2,1,0:T(8,128)(2,1)}, u32[]{:S(2)}) copy-start(bf16[2,192,1024]{2,1,0:T(8,128)(2,1)} %param.16) | copy-start | bytes 2359300
  1270.7 51.9 %copy-start.40 = (f32[1024]{0:T(1024)S(1)}, f32[1024]{0:T(1024)}, u32[]{:S(2)}) copy-start(f32[1024]{0:T(1024)} %param.17) | copy-start | bytes 12292
  1509.9 8.4 copy-start.19
  (30 other events, 110.0 us)
Sparse Core Ops, SparseCore 0:
  9.6 115.6 all-gather.3
  136.9 64.9 all-gather.5
  203.4 56.4 all-gather.7
  869.7 85.9 reduce-scatter.3
  958.5 99.1 reduce-scatter.7
  1059.9 201.7 reduce-scatter.5
  1266.4 243.3 all-reduce.17
where the time goes:
time: 1540 us; the launch traced here: 1530 us
  waiting for transfers between devices  678 us (44%)
  local copies, waits for them, and re-layouts  259 us (17%)
  matrix products  253 us (16%)
  other arithmetic  201 us (13%)
  blocking collectives  87.8 us (6%)
  starting transfers between devices  32.3 us (2%)
    reduce_scatter x1, waiting for transfers between devices, per_device(): lax.psum_scatter(in_weight_part, 'fsdp', scatter_dimension=0, tiled=True)  204 us
    psum x1, waiting for transfers between devices, per_device(): in_total, out_total = lax.psum((in_shard, out_shard), 'seq')  186 us
    all_gather x1, waiting for transfers between devices, per_device(): lax.all_gather(in_weight, 'fsdp', axis=0, tiled=True)  115 us
    another operation x121, other arithmetic  113 us
    dot_general x36, matrix products, ssd_span(): jnp.einsum('hij,jhp->ihp', weights, span_values, precision=lax.Precision....  78.8 us
    reduce_scatter x1, waiting for transfers between devices, per_device(): lax.psum_scatter(out_weight_part, 'fsdp', scatter_dimension=0, tiled=True)  67.9 us
    dot_general x48, matrix products, ssd_span(): products = jnp.dot(span_read, span_write.T, precision=lax.Precision.HIGHEST)  62.2 us
    all_to_all x1, blocking collectives, per_device(): lax.all_to_all(mixed_send, 'seq', split_axis=1, concat_axis=2, tiled=True)  45.6 us
  transfers between devices with their start and end apart: 12, of which 7 were waited for; matrix products, arithmetic and copies ran while one was open for 20% of the time, Pallas kernels for 0%

commit v1 on v0

v1 whole, which is shorter than its diff:
```python
import functools

import jax
import jax.numpy as jnp
from jax import lax
from jax.experimental import pallas as pl
from jax.experimental.pallas import tpu as pltpu
from jax.sharding import PartitionSpec as P

HEADDIM = 64
STATE = 128
CONV = 4
HALO = 16
EXTRA = 16
norm_eps = 1e-05
VMEM_BYTES = 56 * 1024 * 1024
f32 = jnp.float32
bf16 = jnp.bfloat16


def exact(a, b, dims):
    return lax.dot_general(
        a, b, (dims, ((), ())), precision=lax.Precision.HIGHEST, preferred_element_type=f32
    )


NN = ((1,), (0,))
TN = ((0,), (0,))
NT = ((1,), (1,))


def iota(shape, dim):
    return lax.broadcasted_iota(jnp.int32, shape, dim)


def spread_matrix(heads):
    shape = (heads, heads * HEADDIM)
    return (iota(shape, 1) // HEADDIM == iota(shape, 0)).astype(f32)


def sigmoid(v):
    return 1.0 / (1.0 + jnp.exp(-v))


def softplus(v):
    return jnp.maximum(v, 0.0) + jnp.log1p(jnp.exp(-jnp.abs(v)))


def whole(shape):
    return pl.BlockSpec(shape, lambda g: (0,) * len(shape))


def per_seq(shape):
    return pl.BlockSpec((1,) + shape, lambda g: (g,) + (0,) * len(shape))


def per_dest(shape):
    return pl.BlockSpec(
        (shape[0], 1) + shape[1:], lambda g: (0, g) + (0,) * (len(shape) - 1)
    )


def call(body, grid, in_specs, out_specs, out_shape, scratch=(), flops=0, moved=0):
    return pl.pallas_call(
        body,
        grid=(grid,),
        in_specs=in_specs,
        out_specs=out_specs,
        out_shape=out_shape,
        scratch_shapes=list(scratch),
        compiler_params=pltpu.CompilerParams(vmem_limit_bytes=VMEM_BYTES),
        cost_estimate=pl.CostEstimate(flops=flops, bytes_accessed=moved, transcendentals=0),
    )


def front_body(dests, p_ref, cw_ref, cb_ref, dtb_ref, al_ref, conv_ref, dt_ref, cum_ref, send_ref, xw_ref):
    length = conv_ref.shape[1]
    channels = conv_ref.shape[2]
    heads = dt_ref.shape[2]
    inner = heads * HEADDIM
    step = softplus(p_ref[0, HALO:, channels : channels + heads].astype(f32) + dtb_ref[...])
    decay = -step * jnp.exp(al_ref[...])
    lower = (iota((length, length), 0) >= iota((length, length), 1)).astype(f32)
    cum = exact(lower, decay, NN)
    dt_ref[0] = step
    cum_ref[0] = cum
    last = cum[length - 1 :, :]
    weight = jnp.exp(last - cum) * step
    spread = spread_matrix(heads)
    weight_wide = exact(weight, spread, NN)
    last_wide = exact(jnp.broadcast_to(last, (8, heads)), spread, NN)[0:1]
    write_side = None
    for start in list(range(inner, channels, 128)) + list(range(0, inner, 128)):
        cols = slice(start, start + 128)
        joined = p_ref[0, :, cols].astype(f32)
        total = cb_ref[:, cols]
        for tap in range(CONV):
            low = HALO - (CONV - 1) + tap
            total = total + cw_ref[tap : tap + 1, cols] * joined[low : low + length]
        conv_ref[0, :, cols] = total
        if start == inner:
            write_side = total * sigmoid(total)
        elif start < inner:
            xw_ref[:, cols] = total * sigmoid(total) * weight_wide[:, cols]
    state = exact(write_side, xw_ref[...], TN)
    width = send_ref.shape[3]
    hi = last_wide.astype(bf16)
    rest = last_wide - hi.astype(f32)
    mid = rest.astype(bf16)
    low_part = (rest - mid.astype(f32)).astype(bf16)
    row = iota((EXTRA, inner), 0)
    tail = jnp.where(
        row == 0,
        hi.astype(f32),
        jnp.where(row == 1, mid.astype(f32), jnp.where(row == 2, low_part.astype(f32), 0.0)),
    )
    for dest in range(dests):
        cols = slice(dest * width, (dest + 1) * width)
        send_ref[dest, 0, :STATE, :] = state[:, cols].astype(send_ref.dtype)
        send_ref[dest, 0, STATE:, :] = tail[:, cols].astype(send_ref.dtype)


def scan_front(p_ext, conv_weight, conv_bias, dt_bias, a_log, dests, kind):
    seqs, rows, _ = p_ext.shape
    length = rows - HALO
    heads = dt_bias.shape[0]
    inner = heads * HEADDIM
    channels = inner + 2 * STATE
    width = inner // dests
    return call(
        functools.partial(front_body, dests),
        seqs,
        [
            per_seq(p_ext.shape[1:]),
            whole((CONV, channels)),
            whole((1, channels)),
            whole((1, heads)),
            whole((1, heads)),
        ],
        [
            per_seq((length, channels)),
            per_seq((length, heads)),
            per_seq((length, heads)),
            per_dest((dests, STATE + EXTRA, width)),
        ],
        [
            jax.ShapeDtypeStruct((seqs, length, channels), f32),
            jax.ShapeDtypeStruct((seqs, length, heads), f32),
            jax.ShapeDtypeStruct((seqs, length, heads), f32),
            jax.ShapeDtypeStruct((dests, seqs, STATE + EXTRA, width), kind),
        ],
        [pltpu.VMEM((length, inner), f32)],
        flops=12 * seqs * length * STATE * inner,
        moved=seqs * length * channels * 6,
    )(p_ext, conv_weight, conv_bias[None], dt_bias[None], a_log[None])


def combine_body(recv_ref, start_ref, decay_ref):
    dests, seqs, _, width = recv_ref.shape
    for seq in range(seqs):
        state = jnp.zeros((STATE, width), f32)
        for src in range(dests):
            start_ref[src, seq] = state.astype(start_ref.dtype)
            total = recv_ref[src, seq, STATE:, :].astype(f32)
            decay = jnp.exp(total[0:1] + total[1:2] + total[2:3])
            decay_ref[src, seq] = jnp.broadcast_to(decay, (8, width))
            state = decay * state + recv_ref[src, seq, :STATE, :].astype(f32)


def combine(recv):
    dests, seqs, _, width = recv.shape
    return pl.pallas_call(
        combine_body,
        out_shape=[
            jax.ShapeDtypeStruct((dests, seqs, STATE, width), recv.dtype),
            jax.ShapeDtypeStruct((dests, seqs, 8, width), f32),
        ],
        compiler_params=pltpu.CompilerParams(vmem_limit_bytes=VMEM_BYTES),
        cost_estimate=pl.CostEstimate(
            flops=2 * recv.size, bytes_accessed=4 * recv.size, transcendentals=0
        ),
    )(recv)


def combine_back_body(recv_ref, decay_ref, end_ref):
    dests, seqs, _, width = recv_ref.shape
    for seq in range(seqs):
        state = jnp.zeros((STATE, width), f32)
        for src in reversed(range(dests)):
            end_ref[src, seq] = state.astype(end_ref.dtype)
            state = decay_ref[src, seq, 0:1] * state + recv_ref[src, seq].astype(f32)


def combine_back(recv, decay):
    return pl.pallas_call(
        combine_back_body,
        out_shape=jax.ShapeDtypeStruct(recv.shape, recv.dtype),
        compiler_params=pltpu.CompilerParams(vmem_limit_bytes=VMEM_BYTES),
        cost_estimate=pl.CostEstimate(
            flops=2 * recv.size, bytes_accessed=4 * recv.size, transcendentals=0
        ),
    )(recv, decay)


def columns(array):
    length = array.shape[0]
    eye = (iota((length, length), 0) == iota((length, length), 1)).astype(f32)
    return exact(array, eye, TN)


def within_body(conv_ref, dt_ref, cum_ref, y_ref):
    length = conv_ref.shape[1]
    heads = dt_ref.shape[2]
    inner = heads * HEADDIM
    write_conv = conv_ref[0, :, inner : inner + STATE]
    read_conv = conv_ref[0, :, inner + STATE :]
    products = exact(read_conv * sigmoid(read_conv), write_conv * sigmoid(write_conv), NT)
    cum = cum_ref[0]
    cum_t = columns(cum)
    dt_wide = exact(dt_ref[0], spread_matrix(heads), NN)
    causal = iota((length, length), 0) >= iota((length, length), 1)
    left = iota((length, 2 * HEADDIM), 1) < HEADDIM
    for pair in range(heads // 2):
        cols = slice(pair * 2 * HEADDIM, (pair + 1) * 2 * HEADDIM)
        conv = conv_ref[0, :, cols]
        scaled = conv * sigmoid(conv) * dt_wide[:, cols]
        parts = []
        for head in (2 * pair, 2 * pair + 1):
            gap = cum[:, head : head + 1] - cum_t[head : head + 1, :]
            weights = jnp.exp(jnp.where(causal, gap, -1e30)) * products
            parts.append(exact(weights, scaled, NN))
        y_ref[0, :, cols] = jnp.where(left, parts[0], parts[1])


def scan_within(conv, dt, cum):
    seqs, length, channels = conv.shape
    heads = dt.shape[2]
    inner = heads * HEADDIM
    return call(
        within_body,
        seqs,
        [per_seq((length, channels)), per_seq((length, heads)), per_seq((length, heads))],
        per_seq((length, inner)),
        jax.ShapeDtypeStruct((seqs, length, inner), f32),
        flops=24 * seqs * length * length * inner,
        moved=seqs * length * channels * 8,
    )(conv, dt, cum)


def middle_body(
    y_ref, conv_ref, cum_ref, start_ref, gate_ref, gain_ref, skip_ref, gn_ref,
    normed_ref, gg_ref, gm_ref, send_ref, gain_part_ref, gs_ref, skip_part_ref, cread_ref,
    state_ref, scan_ref, gated_ref,
):
    length = conv_ref.shape[1]
    heads = cum_ref.shape[2]
    inner = heads * HEADDIM
    dests, _, _, width = start_ref.shape
    for dest in range(dests):
        state_ref[:, dest * width : (dest + 1) * width] = start_ref[dest, 0].astype(f32)
    read_conv = conv_ref[0, :, inner + STATE :]
    read_side = read_conv * sigmoid(read_conv)
    spread = spread_matrix(heads)
    grow = jnp.exp(cum_ref[0])
    grow_wide = exact(grow, spread, NN)
    skip_wide = exact(jnp.broadcast_to(skip_ref[...], (8, heads)), spread, NN)[0:1]
    scan_ref[...] = exact(read_side, state_ref[...], NN) * grow_wide + y_ref[0]
    square = jnp.zeros((length, 128), f32)
    for start in range(0, inner, 128):
        cols = slice(start, start + 128)
        conv = conv_ref[0, :, cols]
        mixed = scan_ref[:, cols] + skip_wide[:, cols] * (conv * sigmoid(conv))
        mixed = mixed.astype(bf16).astype(f32)
        gate = gate_ref[0, :, cols].astype(f32)
        gated = mixed * (gate * sigmoid(gate))
        gated_ref[:, cols] = gated
        square = square + gated * gated
    inv = lax.rsqrt(jnp.sum(square, axis=1, keepdims=True) / inner + norm_eps)
    cross = jnp.zeros((length, 128), f32)
    for start in range(0, inner, 128):
        cols = slice(start, start + 128)
        gated = gated_ref[:, cols]
        grad = gn_ref[0, :, cols]
        unit = gated * inv
        normed_ref[0, :, cols] = (unit * gain_ref[:, cols]).astype(bf16)
        gain_part_ref[0, :, cols] = jnp.sum(grad * unit, axis=0, keepdims=True)
        cross = cross + gated * (grad * gain_ref[:, cols])
    mean = jnp.sum(cross, axis=1, keepdims=True) / inner
    factor = inv * inv * inv * mean
    for start in range(0, inner, 128):
        cols = slice(start, start + 128)
        conv = conv_ref[0, :, cols]
        values = conv * sigmoid(conv)
        scanned = scan_ref[:, cols]
        mixed = (scanned + skip_wide[:, cols] * values).astype(bf16).astype(f32)
        gate = gate_ref[0, :, cols].astype(f32)
        sig = sigmoid(gate)
        grad_gated = inv * (gain_ref[:, cols] * gn_ref[0, :, cols]) - gated_ref[:, cols] * factor
        gg_ref[0, :, cols] = (grad_gated * mixed * (sig * (1.0 + gate * (1.0 - sig)))).astype(bf16)
        grad_low = (grad_gated * (gate * sig)).astype(bf16)
        gm_ref[0, :, cols] = grad_low
        grad_mixed = grad_low.astype(f32)
        scan_ref[:, cols] = scanned * grad_mixed
        skip_part_ref[0, :, cols] = jnp.sum(values * grad_mixed, axis=0, keepdims=True)
        gated_ref[:, cols] = grad_mixed * grow_wide[:, cols]
    gs_ref[0] = exact(scan_ref[...], spread, NT)
    cread_ref[0] = exact(gated_ref[...], state_ref[...], NT)
    back = exact(read_side, gated_ref[...], TN)
    for dest in range(dests):
        send_ref[dest, 0] = back[:, dest * width : (dest + 1) * width].astype(send_ref.dtype)


def middle(y, conv, cum, start, gate, gate_gain, skip_gain, grad_normed):
    seqs, length, channels = conv.shape
    heads = cum.shape[2]
    inner = heads * HEADDIM
    dests, _, _, width = start.shape
    row = per_seq((length, inner))
    line = per_seq((1, inner))
    return call(
        middle_body,
        seqs,
        [
            row,
            per_seq((length, channels)),
            per_seq((length, heads)),
            per_dest((dests, STATE, width)),
            row,
            whole((1, inner)),
            whole((1, heads)),
            row,
        ],
        [
            row, row, row,
            per_dest((dests, STATE, width)),
            line,
            per_seq((length, heads)),
            line,
            per_seq((length, STATE)),
        ],
        [
            jax.ShapeDtypeStruct((seqs, length, inner), bf16),
            jax.ShapeDtypeStruct((seqs, length, inner), bf16),
            jax.ShapeDtypeStruct((seqs, length, inner), bf16),
            jax.ShapeDtypeStruct(start.shape, start.dtype),
            jax.ShapeDtypeStruct((seqs, 1, inner), f32),
            jax.ShapeDtypeStruct((seqs, length, heads), f32),
            jax.ShapeDtypeStruct((seqs, 1, inner), f32),
            jax.ShapeDtypeStruct((seqs, length, STATE), f32),
        ],
        [
            pltpu.VMEM((STATE, inner), f32),
            pltpu.VMEM((length, inner), f32),
            pltpu.VMEM((length, inner), f32),
        ],
        flops=36 * seqs * length * STATE * inner,
        moved=seqs * length * channels * 20,
    )(y, conv, cum, start, gate, gate_gain[None], skip_gain[None], grad_normed)


def within_back_body(conv_ref, dt_ref, cum_ref, gm_ref, cread_ref, u_ref, dw_ref, dr_ref):
    length = conv_ref.shape[1]
    heads = dt_ref.shape[2]
    inner = heads * HEADDIM
    write_conv = conv_ref[0, :, inner : inner + STATE]
    read_conv = conv_ref[0, :, inner + STATE :]
    write_side = write_conv * sigmoid(write_conv)
    read_side = read_conv * sigmoid(read_conv)
    products = exact(write_side, read_side, NT)
    cum = cum_ref[0]
    cum_t = columns(cum)
    dt_wide = exact(dt_ref[0], spread_matrix(heads), NN)
    causal = iota((length, length), 0) <= iota((length, length), 1)
    left = iota((length, 2 * HEADDIM), 1) < HEADDIM
    grad_products = jnp.zeros((length, length), f32)
    for pair in range(heads // 2):
        cols = slice(pair * 2 * HEADDIM, (pair + 1) * 2 * HEADDIM)
        conv = conv_ref[0, :, cols]
        scaled = conv * sigmoid(conv) * dt_wide[:, cols]
        grad = gm_ref[0, :, cols].astype(f32)
        parts = []
        for side, head in enumerate((2 * pair, 2 * pair + 1)):
            gap = cum_t[head : head + 1, :] - cum[:, head : head + 1]
            decays = jnp.exp(jnp.where(causal, gap, -1e30))
            parts.append(exact(decays * products, grad, NN))
            own = jnp.where(left if side == 0 else ~left, scaled, 0.0)
            grad_products = grad_products + decays * exact(own, grad, NT)
        u_ref[0, :, cols] = jnp.where(left, parts[0], parts[1])
    dw_ref[0] = exact(grad_products, read_side, NN)
    dr_ref[0] = exact(grad_products, write_side, TN) + cread_ref[0]


def scan_within_back(conv, dt, cum, grad_mixed, cread):
    seqs, length, channels = conv.shape
    heads = dt.shape[2]
    inner = heads * HEADDIM
    side = per_seq((length, STATE))
    return call(
        within_back_body,
        seqs,
        [
            per_seq((length, channels)),
            per_seq((length, heads)),
            per_seq((length, heads)),
            per_seq((length, inner)),
            side,
        ],
        [per_seq((length, inner)), side, side],
        [
            jax.ShapeDtypeStruct((seqs, length, inner), f32),
            jax.ShapeDtypeStruct((seqs, length, STATE), f32),
            jax.ShapeDtypeStruct((seqs, length, STATE), f32),
        ],
        flops=48 * seqs * length * length * inner,
        moved=seqs * length * channels * 10,
    )(conv, dt, cum, grad_mixed, cread)


def back_body(
    u_ref, dw_ref, dr_ref, conv_ref, p_ref, dt_ref, cum_ref, gm_ref, gs_ref,
    start_ref, end_ref, cw_ref, dtb_ref, al_ref, skip_ref,
    dconv_ref, ddt_ref, cwp_ref, cbp_ref, dtp_ref, alp_ref,
    state_ref, xw_ref, xu_ref, xs_ref,
):
    length = conv_ref.shape[1]
    channels = conv_ref.shape[2]
    heads = dt_ref.shape[2]
    inner = heads * HEADDIM
    dests, _, _, width = start_ref.shape
    spread = spread_matrix(heads)
    step = dt_ref[0]
    cum = cum_ref[0]
    last = cum[length - 1 :, :]
    weight = jnp.exp(last - cum)
    step_wide = exact(step, spread, NN)
    weight_wide = exact(weight, spread, NN)
    skip_wide = exact(jnp.broadcast_to(skip_ref[...], (8, heads)), spread, NN)[0:1]
    inner_sum = []
    for dest in range(dests):
        cols = slice(dest * width, (dest + 1) * width)
        end = end_ref[dest, 0].astype(f32)
        state_ref[:, cols] = end
        inner_sum.append(jnp.sum(end * start_ref[dest, 0].astype(f32), axis=0, keepdims=True))
    inner_sum = jnp.concatenate(inner_sum, axis=1)
    write_conv = conv_ref[0, :, inner : inner + STATE]
    write_side = write_conv * sigmoid(write_conv)
    xs_ref[...] = exact(write_side, state_ref[...], NN) * weight_wide

    def conv_back(start, grad):
        cols = slice(start, start + 128)
        conv = conv_ref[0, :, cols]
        sig = sigmoid(conv)
        dconv = grad * (sig * (1.0 + conv * (1.0 - sig)))
        dconv_ref[0, :, cols] = dconv
        cbp_ref[0, :, cols] = jnp.sum(dconv, axis=0, keepdims=True)
        joined = p_ref[0, :, cols].astype(f32)
        for tap in range(CONV):
            low = HALO - (CONV - 1) + tap
            cwp_ref[0, tap : tap + 1, cols] = jnp.sum(
                dconv * joined[low : low + length], axis=0, keepdims=True
            )

    for start in range(0, inner, 128):
        cols = slice(start, start + 128)
        conv = conv_ref[0, :, cols]
        values = conv * sigmoid(conv)
        from_state = xs_ref[:, cols]
        total = u_ref[0, :, cols] + from_state
        xu_ref[:, cols] = values * total
        xs_ref[:, cols] = values * from_state
        xw_ref[:, cols] = values * (step_wide[:, cols] * weight_wide[:, cols])
        grad = step_wide[:, cols] * total + skip_wide[:, cols] * gm_ref[0, :, cols].astype(f32)
        conv_back(start, grad)
    conv_back(inner, dw_ref[0] + exact(xw_ref[...], state_ref[...], NT))
    conv_back(inner + STATE, dr_ref[0])
    direct = exact(xu_ref[...], spread, NT)
    ends = exact(xs_ref[...], spread, NT) * step
    held = exact(jnp.broadcast_to(inner_sum, (8, inner)), spread, NT)[0:1] * jnp.exp(last)
    at_end = jnp.sum(ends, axis=0, keepdims=True) + held
    dcum = gs_ref[0] - step * direct
    dcum = dcum + jnp.where(iota((length, heads), 0) == length - 1, at_end, 0.0)
    upper = (iota((length, length), 0) <= iota((length, length), 1)).astype(f32)
    da = exact(upper, dcum, NN)
    rate = jnp.exp(al_ref[...])
    alp_ref[0] = jnp.sum(da * (-step * rate), axis=0, keepdims=True)
    raw = p_ref[0, HALO:, channels : channels + heads].astype(f32) + dtb_ref[...]
    draw = (direct - da * rate) * sigmoid(raw)
    ddt_ref[0] = draw.astype(bf16)
    dtp_ref[0] = jnp.sum(draw, axis=0, keepdims=True)


def scan_back(u, dw, dr, conv, p_ext, dt, cum, gm, gs, start, end, conv_weight, dt_bias, a_log, skip_gain):
    seqs, length, channels = conv.shape
    heads = dt.shape[2]
    inner = heads * HEADDIM
    dests, _, _, width = start.shape
    row = per_seq((length, inner))
    small = per_seq((length, heads))
    side = per_seq((length, STATE))
    states = per_dest((dests, STATE, width))
    return call(
        back_body,
        seqs,
        [
            row, side, side,
            per_seq((length, channels)),
            per_seq(p_ext.shape[1:]),
            small, small, row, small, states, states,
            whole((CONV, channels)),
            whole((1, heads)),
            whole((1, heads)),
            whole((1, heads)),
        ],
        [
            per_seq((length, channels)),
            small,
            per_seq((CONV, channels)),
            per_seq((1, channels)),
            per_seq((1, heads)),
            per_seq((1, heads)),
        ],
        [
            jax.ShapeDtypeStruct((seqs, length, channels), f32),
            jax.ShapeDtypeStruct((seqs, length, heads), bf16),
            jax.ShapeDtypeStruct((seqs, CONV, channels), f32),
            jax.ShapeDtypeStruct((seqs, 1, channels), f32),
            jax.ShapeDtypeStruct((seqs, 1, heads), f32),
            jax.ShapeDtypeStruct((seqs, 1, heads), f32),
        ],
        [
            pltpu.VMEM((STATE, inner), f32),
            pltpu.VMEM((length, inner), f32),
            pltpu.VMEM((length, inner), f32),
            pltpu.VMEM((length, inner), f32),
        ],
        flops=24 * seqs * length * STATE * inner,
        moved=seqs * length * channels * 24,
    )(u, dw, dr, conv, p_ext, dt, cum, gm, gs, start, end, conv_weight,
      dt_bias[None], a_log[None], skip_gain[None])


def swap(x, axis, flip):
    count = lax.axis_size(axis)
    return lax.ppermute(x, axis, [(slot, slot ^ flip) for slot in range(count)])


def total_over_all(x):
    for axis in ("seq", "fsdp"):
        flip = 1
        while flip < lax.axis_size(axis):
            x = x + swap(x, axis, flip)
            flip *= 2
    return x


def shared_slots():
    slot = lax.axis_index("seq")
    return slot // 4, slot // 2 % 2 == 1, slot % 2 == 1, lax.axis_index("fsdp") == 1


def fast_mesh():
    return lax.axis_size("fsdp") == 2 and lax.axis_size("seq") == 16


def halves(x, flag, axis):
    size = x.shape[axis] // 2
    low = lax.slice_in_dim(x, 0, size, axis=axis)
    high = lax.slice_in_dim(x, size, 2 * size, axis=axis)
    return jnp.where(flag, high, low), jnp.where(flag, low, high)


def join(own, other, flag, axis):
    low = jnp.where(flag, other, own)
    high = jnp.where(flag, own, other)
    return jnp.concatenate([low, high], axis=axis)


def fetch_rows(w):
    _, _, odd, _ = shared_slots()
    mine, _ = halves(w, odd, 0)
    fetched = swap(mine, "fsdp", 1)
    return fetched, swap(fetched, "seq", 1)


def gather_rows(w):
    if not fast_mesh():
        return lax.all_gather(w, "fsdp", axis=0, tiled=True)
    _, _, odd, second = shared_slots()
    fetched, shared = fetch_rows(w)
    return join(w, join(fetched, shared, odd, 0), second, 0)


def reduce_rows(part):
    shard = lax.psum_scatter(part, "fsdp", scatter_dimension=0, tiled=True)
    return lax.psum(shard, "seq")


def fold(total, axis, flip, dim):
    size = total.shape[dim] // 2
    keep = lax.slice_in_dim(total, 0, size, axis=dim)
    give = lax.slice_in_dim(total, size, 2 * size, axis=dim)
    return keep + swap(give.astype(bf16), axis, flip).astype(f32)


def ring(x, shift):
    return lax.ppermute(x, "seq", [(slot, (slot + 4 * shift) % 16) for slot in range(16)])


def scatter_z(total, z):
    size = total.shape[0] // 4
    mine = lax.dynamic_slice_in_dim(total, z * size, size, 0)
    for shift in range(1, 4):
        give = lax.dynamic_slice_in_dim(total, (z + shift) % 4 * size, size, 0)
        mine = mine + ring(give.astype(bf16), shift).astype(f32)
    return mine


def gather_z(mine, z):
    size = mine.shape[0]
    total = jnp.zeros((4 * size,) + mine.shape[1:], mine.dtype)
    total = lax.dynamic_update_slice_in_dim(total, mine, z * size, 0)
    for shift in range(1, 4):
        total = lax.dynamic_update_slice_in_dim(
            total, ring(mine, shift), (z - shift) % 4 * size, 0
        )
    return total


def spread_total(mine):
    z, x, odd, _ = shared_slots()
    total = gather_z(mine.astype(bf16), z)
    total = join(total, swap(total, "seq", 2), x, 1)
    return join(total, swap(total, "seq", 1), odd, 1)


def dot(a, b, dims):
    return lax.dot_general(a, b, (dims, ((), ())), preferred_element_type=f32)


STATE_TYPE = bf16


def per_device(
    hidden_in, cotangent, norm_gain, in_weight, conv_weight, conv_bias,
    dt_bias, a_log, skip_gain, gate_gain, out_weight,
):
    seq_count = lax.axis_size("seq")
    seqs, length, width = hidden_in.shape
    rows = seqs * length
    heads = dt_bias.shape[0]
    inner = heads * HEADDIM
    forward = [(slot, slot + 1) for slot in range(seq_count - 1)]
    backward = [(slot + 1, slot) for slot in range(seq_count - 1)]

    w_gate, w_scan = in_weight[:, :inner], in_weight[:, inner:]
    halo = lax.ppermute(hidden_in[:, length - HALO :], "seq", forward)
    fast = fast_mesh()
    if fast:
        z, x, odd, second = shared_slots()
        scan_fetched, scan_shared = fetch_rows(w_scan)
    else:
        scan_full = gather_rows(w_scan)

    def prenorm(rows_in):
        inv = lax.rsqrt(jnp.mean(rows_in * rows_in, axis=-1, keepdims=True) + norm_eps)
        return inv, (rows_in * inv * norm_gain).astype(bf16)

    residual = hidden_in.astype(f32)
    inv_rms, scaled_low = prenorm(residual)
    _, scaled_halo = prenorm(halo.astype(f32))
    scaled_ext = jnp.concatenate([scaled_halo, scaled_low], axis=1)
    scaled_low = scaled_low.reshape(rows, width)
    scaled_ext = scaled_ext.reshape(seqs * (HALO + length), width)
    if fast:
        ext_own, ext_other = halves(scaled_ext, second, 1)
        ext_fetched, ext_shared = halves(ext_other, odd, 1)
        p_ext = dot(ext_own, w_scan, NN) + dot(ext_fetched, scan_fetched, NN)
        p_ext = p_ext + dot(ext_shared, scan_shared, NN)
    else:
        p_ext = dot(scaled_ext, scan_full, NN)
    p_ext = p_ext.astype(bf16).reshape(seqs, HALO + length, -1)
    conv, dt, cum, send = scan_front(
        p_ext, conv_weight, conv_bias, dt_bias, a_log, seq_count, STATE_TYPE
    )
    recv = lax.all_to_all(send, "seq", split_axis=0, concat_axis=0, tiled=True)
    w_gate, w_out, _ = lax.optimization_barrier((w_gate, out_weight, p_ext))
    gate_full = gather_rows(w_gate)
    out_full = gather_rows(w_out)
    y = scan_within(conv, dt, cum)
    start_heads, decay = combine(recv)
    start = lax.all_to_all(start_heads, "seq", split_axis=0, concat_axis=0, tiled=True)
    gate = dot(scaled_low, gate_full, NN).astype(bf16).reshape(seqs, length, inner)
    grad_rows = cotangent.reshape(rows, width)
    grad_normed = dot(grad_rows, out_full, NT).reshape(seqs, length, inner)
    normed, grad_gate, grad_mixed, back_send, gain_part, gs, skip_part, cread = middle(
        y, conv, cum, start, gate, gate_gain, skip_gain, grad_normed
    )
    back_recv = lax.all_to_all(back_send, "seq", split_axis=0, concat_axis=0, tiled=True)
    u, dw, dr = scan_within_back(conv, dt, cum, grad_mixed, cread)
    end_heads = combine_back(back_recv, decay)
    end = lax.all_to_all(end_heads, "seq", split_axis=0, concat_axis=0, tiled=True)
    normed = normed.reshape(rows, inner)
    grad_gate = grad_gate.reshape(rows, inner)
    hidden_out = (residual.reshape(rows, width) + dot(normed, out_full, NN)).astype(bf16)
    if fast:
        scan_full = join(w_scan, join(scan_fetched, scan_shared, odd, 0), second, 0)
        own_side, other_side = halves(scaled_low, second, 1)
        quarters = [halves(side, odd, 1) for side in (own_side, other_side)]
        eighths = [[halves(quarter, x, 1) for quarter in pair] for pair in quarters]
        by_y = [
            jnp.concatenate([eighths[y][c][k] for y in (0, 1) for k in (0, 1)], axis=1)
            for c in (0, 1)
        ]
        by_x = [
            jnp.concatenate([eighths[y][c][k] for k in (0, 1) for y in (0, 1)], axis=1)
            for c in (0, 1)
        ]

        def near(left, right):
            keep = dot(left, right[0], TN)
            give = dot(left, right[1], TN).astype(bf16)
            return keep + swap(give, "seq", 1).astype(f32)

        def reduce_y(left):
            total = fold(fold(near(left, by_y), "fsdp", 1, 1), "seq", 2, 1)
            return spread_total(scatter_z(total, z))

        def reduce_x(left):
            total = fold(fold(near(left, by_x), "seq", 2, 1), "fsdp", 1, 1)
            return spread_total(scatter_z(total, z))

        sides = [halves(side, x, 1) for side in halves(grad_rows, odd, 1)]
        cot = [jnp.concatenate(side, axis=1) for side in sides]
        total = near(jnp.concatenate(halves(normed, second, 1), axis=1), cot)
        total = fold(fold(total, "seq", 2, 1), "fsdp", 1, 0)
        out_total = spread_total(scatter_z(total, z)).astype(f32)
        gate_total = reduce_y(grad_gate)
    else:
        out_total = reduce_rows(dot(normed, grad_rows, TN))
        gate_total = reduce_rows(dot(scaled_low, grad_gate, TN))
    dconv, ddt, conv_part, bias_part, shift_part, rate_part = scan_back(
        u, dw, dr, conv, p_ext, dt, cum, grad_mixed, gs, start, end,
        conv_weight, dt_bias, a_log, skip_gain,
    )
    after = lax.ppermute(dconv[:, :8], "seq", backward)
    dconv = jnp.concatenate([dconv, after], axis=1)
    grad_joined = jnp.zeros(conv.shape, f32)
    for tap in range(CONV):
        low = CONV - 1 - tap
        grad_joined = grad_joined + conv_weight[tap] * dconv[:, low : low + length]
    grad_scan = jnp.concatenate([grad_joined.astype(bf16), ddt], axis=2).reshape(rows, -1)
    if fast:
        cut = grad_scan.shape[1] // 64 * 32
        pieces = [gate_total, reduce_y(grad_scan[:, :cut]), reduce_x(grad_scan[:, cut:])]
        in_total = jnp.concatenate(pieces, axis=0).astype(f32).T
    else:
        in_total = jnp.concatenate(
            [gate_total, reduce_rows(dot(scaled_low, grad_scan, TN))], axis=1
        )
    grad_scaled = dot(grad_gate, gate_full, NT) + dot(grad_scan, scan_full, NT)
    residual = residual.reshape(rows, width)
    inv_rms = inv_rms.reshape(rows, 1)
    norm_part = jnp.sum(grad_scaled * residual * inv_rms, axis=0)
    f = norm_gain * grad_scaled
    mean = jnp.mean(residual * f, axis=-1, keepdims=True)
    grad_hidden = (
        grad_rows.astype(f32) + inv_rms * f - residual * (inv_rms * inv_rms * inv_rms * mean)
    )
    skip_heads = jnp.sum(skip_part.reshape(seqs, heads, HEADDIM), axis=(0, 2))
    pieces = [
        norm_part,
        jnp.sum(conv_part, axis=0).reshape(-1),
        jnp.sum(bias_part, axis=(0, 1)),
        jnp.sum(shift_part, axis=(0, 1)),
        jnp.sum(rate_part, axis=(0, 1)),
        skip_heads,
        jnp.sum(gain_part, axis=(0, 1)),
    ]
    sums = total_over_all(jnp.concatenate(pieces))
    parts, at = [], 0
    for piece in pieces:
        parts.append(sums[at : at + piece.shape[0]])
        at += piece.shape[0]
    norm_sum, conv_sum, bias_sum, shift_sum, rate_sum, skip_sum, gain_sum = parts
    return (
        hidden_out.reshape(hidden_in.shape),
        grad_hidden.reshape(hidden_in.shape),
        norm_sum,
        in_total,
        conv_sum.reshape(conv_weight.shape),
        bias_sum,
        shift_sum,
        rate_sum,
        skip_sum,
        gain_sum,
        out_total,
    )


def solution(mesh):
    tokens = P("fsdp", "seq", None)
    weights = P("fsdp", None)
    return jax.shard_map(
        per_device,
        mesh=mesh,
        in_specs=(tokens, tokens, P(), weights, P(), P(), P(), P(), P(), P(), weights),
        out_specs=(tokens, tokens, P(), weights, P(), P(), P(), P(), P(), P(), weights),
        check_vma=False,
    )
```

time: 1540 us -> 519 us (0.34)
  waiting for transfers between devices: 678 us -> 155 us
  matrix products: 253 us -> 40.8 us
  local copies, waits for them, and re-layouts: 259 us -> 51.2 us
  other arithmetic: 201 us -> 71 us
  Pallas kernels: 0 us -> 103 us
  blocking collectives: 87.8 us -> 0 us
  starting transfers between devices: 32.3 us -> 88.8 us
    reduce_scatter x3 -> x0, waiting for transfers between devices: 272 us -> none  [the longest x1 204 us: per_device(): lax.psum_scatter(in_weight_part, 'fsdp', scatter_dimension=0, tiled=True)]
    dot_general x150 -> x16, matrix products: 232 us -> 40.8 us  [dot(): return lax.dot_general(a, b, (dims, ((), ())), preferred_element_type=f32)]
    psum x1 -> x0, waiting for transfers between devices: 186 us -> none  [per_device(): in_total, out_total = lax.psum((in_shard, out_shard), 'seq')]
    ppermute x0 -> x57, waiting for transfers between devices: none -> 144 us  [the longest x31 123 us: swap(): return lax.ppermute(x, axis, [(slot, slot ^ flip) for slot in range(count)])]
    all_gather x3 -> x0, waiting for transfers between devices: 115 us -> none  [the longest x1 115 us: per_device(): lax.all_gather(in_weight, 'fsdp', axis=0, tiled=True)]
    another operation x133 -> x0, other arithmetic: 113 us -> none
    pallas_call x0 -> x7, Pallas kernels: none -> 103 us  [the longest x1 27.4 us: scan_within_back(): call(within_back_body, seqs, [per_seq((length, channels)), per_seq((lengt...]
    reshape x32 -> x2, local copies, waits for them, and re-layouts: 95.3 us -> 2.02 us  [the longest x1 1.39 us: per_device(): jnp.sum(conv_part, axis=0).reshape(-1)]
  transfers between devices with their start and end apart: 12 -> 61, of which waited for: 7 -> 21; matrix products, arithmetic and copies ran while one was open for 20% -> 23% of each run, Pallas kernels for 0% -> 16%
where the time goes in v1:
time: 519 us; the launch traced here: 512 us
  waiting for transfers between devices  155 us (30%)
  Pallas kernels  103 us (20%)
  starting transfers between devices  88.8 us (17%)
  other arithmetic  71 us (14%)
  local copies, waits for them, and re-layouts  51.2 us (10%)
  matrix products  40.8 us (8%)
    ppermute x31, waiting for transfers between devices, swap(): return lax.ppermute(x, axis, [(slot, slot ^ flip) for slot in range(count)])  123 us
    dot_general x16, matrix products, dot(): return lax.dot_general(a, b, (dims, ((), ())), preferred_element_type=f32)  40.8 us
    ppermute x24, starting transfers between devices, ring(): lax.ppermute(x, 'seq', [(slot, (slot + 4 * shift) % 16) for slot in range...  37.4 us
    pallas_call x1, Pallas kernels, scan_within_back(): call(within_back_body, seqs, [per_seq((length, channels)), per_seq((lengt...  27.4 us
    ppermute x31, starting transfers between devices, swap(): return lax.ppermute(x, axis, [(slot, slot ^ flip) for slot in range(count)])  24.8 us
    pallas_call x1, Pallas kernels, scan_back(): call(back_body, seqs, [row, side, side, per_seq((length, channels)), per_...  24 us
    transpose x1, other arithmetic, per_device(): in_total = jnp.concatenate(pieces, axis=0).astype(f32).T  23.1 us
    ppermute x24, waiting for transfers between devices, ring(): lax.ppermute(x, 'seq', [(slot, (slot + 4 * shift) % 16) for slot in range...  20.7 us
  transfers between devices with their start and end apart: 61, of which 21 were waited for; matrix products, arithmetic and copies ran while one was open for 23% of the time, Pallas kernels for 16%

profile of v1, /device:TPU:0, one launch (start us, length us, event | category | flops | bytes accessed | tf_op | source)
XLA Modules:
  0.0 511.7 jit_solution(5345696629712242731)
XLA Ops:
  2.2 2.3 collective-permute-start
  4.6 2.8 slice_select_fusion
  7.4 2.3 collective-permute-start.1
  14.2 21.8 %collective-permute-done.1 = bf16[256,2336]{0,1:T(8,128)(2,1)} collective-permute-done((bf16[256,2336]{0,1:T(8,128)(2,1)}, bf16[256,2336]{0,1:T(8,128)(2,1)}, u32[]{:S(2)}, u32[]{:S(2)}) %collective-permute-start.1) | collective-permute-done | bytes 1196064 | tf_op jit(solution)/shard_map/ppermute | solution.py:544
  38.4 2.1 convolution_add_fusion.1
  40.5 2.1 fusion.4
  43.7 2.0 collective-permute-start.3
  47.7 10.5 %shard_map.194 = (f32[2,192,2304]{2,1,0:T(8,128)}, f32[2,192,32]{2,1,0:T(8,128)}, f32[2,192,32]{2,1,0:T(8,128)}, bf16[16,2,144,128]{3,2,1,0:T(8,128)(2,1)}) custom-call(bf16[2,208,2336]{2,1,0:T(8,128)(2,1)} %bitcast.46, f32[4,2304]{1,0:T(4,128)} %cw_ref.3, f32[1,2304]{1,0:T(1,128)} %broadcast_in_dim.36.cb_ref, f32[1,32]{1,0:T(1,128)} %bitcast.65, ...), custom_call_target="tpu_custom_call" | custom-call | flops 1207959552 | bytes 5308416 | tf_op jit(solution)/shard_map/pallas_call | solution.py:130
  58.2 5.7 %all-to-all-start = ((bf16[16,2,144,128]{3,2,1,0:T(8,128)(2,1)}), bf16[16,2,144,128]{3,2,1,0:T(8,128)(2,1)}, u32[]{:S(2)}, u32[]{:S(2)}) async-start(bf16[16,2,144,128]{3,2,1,0:T(8,128)(2,1)} %get-tuple-element.39), calls=%async_computation | async-start | bytes 2359296 | tf_op jit(solution)/shard_map/all_to_all | solution.py:685
  65.9 4.1 collective-permute-done.3
  70.8 21.0 %collective-permute-done.5 = bf16[512,1024]{1,0:T(8,128)(2,1)} collective-permute-done((bf16[512,1024]{1,0:T(8,128)(2,1)}, bf16[512,1024]{1,0:T(8,128)(2,1)}, u32[]{:S(2)}, u32[]{:S(2)}) %collective-permute-start.5) | collective-permute-done | bytes 1048608 | tf_op jit(solution)/shard_map/ppermute | solution.py:544
  93.3 16.1 %shard_map.195.y_ref = f32[2,192,2048]{2,1,0:T(8,128)} custom-call(f32[2,192,2304]{2,1,0:T(8,128)} %get-tuple-element.36.conv_ref, f32[2,192,32]{2,1,0:T(8,128)} %get-tuple-element.37.dt_ref, f32[2,192,32]{2,1,0:T(8,128)} %get-tuple-element.38.cum_ref), custom_call_target="tpu_custom_call" | custom-call | flops 3623878656 | bytes 7077888 | tf_op jit(solution)/shard_map/pallas_call | solution.py:239
  109.4 3.0 broadcast_select_fusion.15
  112.4 2.6 shard_map.196
  115.0 5.7 %all-to-all-start.1 = ((bf16[16,2,128,128]{3,2,1,0:T(8,128)(2,1)}), bf16[16,2,128,128]{3,2,1,0:T(8,128)(2,1)}, u32[]{:S(2)}, u32[]{:S(2)}) async-start(bf16[16,2,128,128]{3,2,1,0:T(8,128)(2,1)} %get-tuple-element.40), calls=%async_computation.1 | async-start | bytes 2097152 | tf_op jit(solution)/shard_map/all_to_all | solution.py:691
  126.1 3.0 convolution_convert_fusion.4
  129.1 3.5 fusion.10
  132.6 11.0 %all-to-all-done.1.start_ref = bf16[16,2,128,128]{3,2,1,0:T(8,128)(2,1)} async-done(((bf16[16,2,128,128]{3,2,1,0:T(8,128)(2,1)}), bf16[16,2,128,128]{3,2,1,0:T(8,128)(2,1)}, u32[]{:S(2)}, u32[]{:S(2)}) %all-to-all-start.1) | async-done | bytes 1048608 | tf_op jit(solution)/shard_map/all_to_all | solution.py:691
  143.6 20.1 %shard_map.197 = (bf16[2,192,2048]{2,1,0:T(8,128)(2,1)}, bf16[2,192,2048]{2,1,0:T(8,128)(2,1)}, bf16[2,192,2048]{2,1,0:T(8,128)(2,1)}, bf16[16,2,128,128]{3,2,1,...) custom-call(f32[2,192,2048]{2,1,0:T(8,128)} %shard_map.195.y_ref, ...), custom_call_target="tpu_custom_call" | custom-call | flops 3623878656 | bytes 17694720 | tf_op jit(solution)/shard_map/pallas_call | solution.py:320
  163.8 4.1 convolution_convert_fusion.3
  169.0 2.6 convolution_convert_fusion
  173.8 3.3 broadcast_select_fusion.1
  177.0 6.5 %all-to-all-start.2 = ((bf16[16,2,128,128]{3,2,1,0:T(8,128)(2,1)}), bf16[16,2,128,128]{3,2,1,0:T(8,128)(2,1)}, u32[]{:S(2)}, u32[]{:S(2)}) async-start(bf16[16,2,128,128]{3,2,1,0:T(8,128)(2,1)} %get-tuple-element.51), calls=%async_computation.2 | async-start | bytes 2097152 | tf_op jit(solution)/shard_map/all_to_all | solution.py:698
  183.7 3.4 convert_add_fusion.1
  191.8 27.4 %shard_map.198 = (f32[2,192,2048]{2,1,0:T(8,128)}, f32[2,192,128]{2,1,0:T(8,128)}, f32[2,192,128]{2,1,0:T(8,128)}) custom-call(f32[2,192,2304]{2,1,0:T(8,128)} %get-tuple-element.36.conv_ref, f32[2,192,32]{2,1,0:T(8,128)} %get-tuple-element.37.dt_ref, f32[2,192,32]{2,1,0:T(8,128)} %get-tuple-element.38.cum_ref, ...), custom_call_target="tpu_custom_call" | custom-call | flops 7247757312 | bytes 8847360 | tf_op jit(solution)/shard_map/pallas_call | solution.py:398
  220.6 2.8 convert_add_fusion
  228.5 2.7 fusion.17
  231.2 2.4 shard_map.199
  233.6 4.9 all-to-all-start.3
  238.5 2.3 slice_add_fusion.1
  242.9 16.5 %collective-permute-done.47 = bf16[2048,256]{0,1:T(8,128)(2,1)S(1)} collective-permute-done((bf16[2048,256]{0,1:T(8,128)(2,1)}, bf16[2048,256]{0,1:T(8,128)(2,1)S(1)}, u32[]{:S(2)}, u32[]{:S(2)}) %collective-permute-start.47) | collective-permute-done | bytes 1048608 | tf_op jit(solution)/shard_map/ppermute | solution.py:544
  260.4 14.0 %collective-permute-done.15 = bf16[2048,128]{0,1:T(8,128)(2,1)S(1)} collective-permute-done((bf16[2048,128]{0,1:T(8,128)(2,1)S(1)}, bf16[2048,128]{0,1:T(8,128)(2,1)S(1)}, u32[]{:S(2)}, u32[]{:S(2)}) %collective-permute-start.15) | collective-permute-done | bytes 524320 | tf_op jit(solution)/shard_map/ppermute | solution.py:544
  274.6 3.5 collective-permute-start.18
  279.5 2.8 collective-permute-start.51
  283.4 3.1 collective-permute-start.49
  286.5 10.7 %collective-permute-done.17 = bf16[512,128]{0,1:T(8,128)(2,1)S(1)} collective-permute-done((bf16[512,128]{0,1:T(8,128)(2,1)S(1)}, bf16[512,128]{0,1:T(8,128)(2,1)S(1)}, u32[]{:S(2)}, u32[]{:S(2)}) %collective-permute-start.17) | collective-permute-done | bytes 131104 | tf_op jit(solution)/shard_map/ppermute | solution.py:606
  299.6 3.2 collective-permute-start.21
  310.7 24.0 %shard_map.200 = (f32[2,192,2304]{2,1,0:T(8,128)}, bf16[2,192,32]{2,1,0:T(8,128)(2,1)}, f32[2,4,2304]{2,1,0:T(4,128)}, f32[2,1,2304]{2,1,0:T(1,128)}, f32[2,1,32]{2,1,0:T(1,128)}, /*index=5*/f32[2,1,32]{2,1,0:T(1,128)}) custom-call(f32[2,192,2048]{2,1,0:T(8,128)} %get-tuple-element.47.u_ref, f32[2,192,128]{2,1,0:T(8,128)} %get-tuple-element.48.dw_ref, ...), custom_call_target="tpu_custom_call" | custom-call | flops 2415919104 | bytes 21233664 | tf_op jit(solution)/shard_map/pallas_call | solution.py:501
  334.7 4.2 constant_dynamic-update-slice_fusion.17
  338.9 2.9 collective-permute-start.54
  360.1 2.1 collective-permute-start.22
  372.0 5.9 %fusion.7 = bf16[2,192,2304]{2,1,0:T(8,128)(2,1)S(1)} fusion(f32[2,200,2304]{2,1,0:T(8,128)} %constant_dynamic-update-slice_fusion.16, f32[2,192,2304]{2,1,0:T(8,128)S(1)} %copy-done.4, f32[2304]{0:T(1024)} %get-tuple-element.65, f32[2304]{0:T(1024)} %get-tuple-element.66, f32[2304]{0:T(1024)} %get-tuple-element.64, f32[2304]{0:T(1024)S(1)} %get-tuple-element.63), kind=kLoop, calls=%fused_computation.15 | loop fusion | flops 7077888 | bytes 15962112 | tf_op jit(solution)/shard_map/convert_element_type | solution.py:751
  379.6 2.2 fusion
  382.6 3.1 fusion.21
  390.7 11.7 %collective-permute-done.9 = f32[14688]{0:T(1024)S(1)} collective-permute-done((f32[14688]{0:T(1024)S(1)}, f32[14688]{0:T(1024)S(1)}, u32[]{:S(2)}, u32[]{:S(2)}) %collective-permute-start.9) | collective-permute-done | bytes 58784 | tf_op jit(solution)/shard_map/ppermute | solution.py:544
  404.3 2.4 collective-permute-done.10
  408.3 3.7 collective-permute-done.11
  414.2 2.1 collective-permute-done.12
  422.7 2.1 convert_add_fusion.3
  425.5 2.1 convert_add_fusion.2
  428.9 11.3 %collective-permute-done.25 = bf16[1152,256]{1,0:T(8,128)(2,1)S(1)} collective-permute-done((bf16[1152,256]{1,0:T(8,128)(2,1)S(1)}, bf16[1152,256]{1,0:T(8,128)(2,1)S(1)}, u32[]{:S(2)}, u32[]{:S(2)}) %collective-permute-start.25) | collective-permute-done | bytes 589856 | tf_op jit(solution)/shard_map/ppermute | solution.py:544
  440.9 2.9 collective-permute-done.36
  444.0 2.1 collective-permute-start.37
  446.1 3.3 collective-permute-done.26
  452.7 2.3 collective-permute-start.40
  457.0 3.2 collective-permute-done.28
  461.1 2.1 collective-permute-start.31
  463.2 2.8 collective-permute-start.32
  468.8 2.8 collective-permute-start.43
  474.2 2.1 collective-permute-done.42
  476.8 4.9 collective-permute-done.33
  481.9 3.0 collective-permute-done.44
  485.1 2.6 maximum_convert_fusion
  488.3 23.1 %convert_bitcast_fusion = f32[512,4384]{0,1:T(8,128)} fusion(bf16[1184,256]{1,0:T(8,128)(2,1)S(1)} %get-tuple-element.90, bf16[1184,256]{1,0:T(8,128)(2,1)S(1)} %get-tuple-element.89, bf16[1152,256]{1,0:T(8,128)(2,1)S(1)} %get-tuple-element.92, bf16[1152,256]{1,0:T(8,128)(2,1)S(1)} %get-tuple-element.91, bf16[2048,256]{1,0:T(8,128)(2,1)S(1)} %get-tuple-element.82, ...), kind=kLoop, calls=%fused_computation | loop fusion | flops 26935296 | bytes 13467648 | tf_op jit(solution)/shard_map/transpose | solution.py:755
  (350 shorter events, 114.2 us)
Async XLA Ops:
  2.2 11.8 %collective-permute-start = (bf16[2,16,1024]{2,1,0:T(8,128)(2,1)}, bf16[2,16,1024]{2,1,0:T(8,128)(2,1)S(1)}, u32[]{:S(2)}, u32[]{:S(2)}) collective-permute-start(bf16[2,16,1024]{2,1,0:T(8,128)(2,1)} %slice.214), channel_id=1, source_target_pairs={{0,2},{2,4},{4,6},{6,8},{8,10},{10,12},{12,14},{14,16},{16,18},{18... | collective-permute-start | bytes 196616 | tf_op jit(solution)/shard_map/ppermute | solution.py:656
  7.4 28.6 %collective-permute-start.1 = (bf16[256,2336]{0,1:T(8,128)(2,1)}, bf16[256,2336]{0,1:T(8,128)(2,1)}, u32[]{:S(2)}, u32[]{:S(2)}) collective-permute-start(bf16[256,2336]{0,1:T(8,128)(2,1)} %slice_select_fusion), channel_id=1, source_target_pairs={{0,1},{1,0},{2,3},{3,2},{4,5},{5,4},{6,7},{7,6},{8,9},{9,8},{10,11... | collective-permute-start | bytes 3588104 | tf_op jit(solution)/shard_map/ppermute | solution.py:544
  36.0 4.5 collective-permute-start.2
  43.7 26.3 %collective-permute-start.3 = (bf16[256,2048]{0,1:T(8,128)(2,1)}, bf16[256,2048]{0,1:T(8,128)(2,1)}, u32[]{:S(2)}, u32[]{:S(2)}) collective-permute-start(bf16[256,2048]{0,1:T(8,128)(2,1)} %slice_select_fusion.2), channel_id=1, source_target_pairs={{0,1},{1,0},{2,3},{3,2},{4,5},{5,4},{6,7},{7,6},{8,9},{9,8},{10,11... | collective-permute-start | bytes 3145736 | tf_op jit(solution)/shard_map/ppermute | solution.py:544
  47.5 44.3 %collective-permute-start.5 = (bf16[512,1024]{1,0:T(8,128)(2,1)}, bf16[512,1024]{1,0:T(8,128)(2,1)}, u32[]{:S(2)}, u32[]{:S(2)}) collective-permute-start(bf16[512,1024]{1,0:T(8,128)(2,1)} %slice_select_fusion.1), channel_id=1, source_target_pairs={{0,1},{1,0},{2,3},{3,2},{4,5},{5,4},{6,7},{7,6},{8,9},{9,8},{10,11... | collective-permute-start | bytes 3145736 | tf_op jit(solution)/shard_map/ppermute | solution.py:544
  58.2 54.2 %all-to-all-start = ((bf16[16,2,144,128]{3,2,1,0:T(8,128)(2,1)}), bf16[16,2,144,128]{3,2,1,0:T(8,128)(2,1)}, u32[]{:S(2)}, u32[]{:S(2)}) async-start(bf16[16,2,144,128]{3,2,1,0:T(8,128)(2,1)} %get-tuple-element.39), calls=%async_computation | async-start | bytes 2359296 | tf_op jit(solution)/shard_map/all_to_all | solution.py:685
  70.0 39.4 %collective-permute-start.4 = (bf16[256,2048]{0,1:T(8,128)(2,1)}, bf16[256,2048]{0,1:T(8,128)(2,1)}, u32[]{:S(2)}, u32[]{:S(2)}) collective-permute-start(bf16[256,2048]{0,1:T(8,128)(2,1)} %collective-permute-done.3), channel_id=1, source_target_pairs={{0,2},{2,0},{4,6},{6,4},{8,10},{10,8},{12,14},{14,12},{16,18},{18,... | collective-permute-start | bytes 3145736 | tf_op jit(solution)/shard_map/ppermute | solution.py:544
  70.0 113.6 %copy-start.36 = (bf16[384,128]{1,0:T(8,128)(2,1)}, bf16[384,128]{1,0:T(8,128)(2,1)S(1)}, u32[]{:S(2)}) copy-start(bf16[384,128]{1,0:T(8,128)(2,1)S(1)} %get-tuple-element.125) | copy-start | bytes 294916
  70.0 113.6 %copy-start.38 = (bf16[384,128]{1,0:T(8,128)(2,1)}, bf16[384,128]{1,0:T(8,128)(2,1)S(1)}, u32[]{:S(2)}) copy-start(bf16[384,128]{1,0:T(8,128)(2,1)S(1)} %get-tuple-element.126) | copy-start | bytes 294916
  91.9 28.8 %collective-permute-start.6 = (bf16[512,1024]{1,0:T(8,128)(2,1)}, bf16[512,1024]{1,0:T(8,128)(2,1)}, u32[]{:S(2)}, u32[]{:S(2)}) collective-permute-start(bf16[512,1024]{1,0:T(8,128)(2,1)} %collective-permute-done.5), channel_id=1, source_target_pairs={{0,2},{2,0},{4,6},{6,4},{8,10},{10,8},{12,14},{14,12},{16,18},{18,... | collective-permute-start | bytes 3145736 | tf_op jit(solution)/shard_map/ppermute | solution.py:544
  91.9 91.8 %copy-start.40 = (bf16[384,128]{1,0:T(8,128)(2,1)}, bf16[384,128]{1,0:T(8,128)(2,1)S(1)}, u32[]{:S(2)}) copy-start(bf16[384,128]{1,0:T(8,128)(2,1)S(1)} %get-tuple-element.127) | copy-start | bytes 294916
  115.0 28.7 %all-to-all-start.1 = ((bf16[16,2,128,128]{3,2,1,0:T(8,128)(2,1)}), bf16[16,2,128,128]{3,2,1,0:T(8,128)(2,1)}, u32[]{:S(2)}, u32[]{:S(2)}) async-start(bf16[16,2,128,128]{3,2,1,0:T(8,128)(2,1)} %get-tuple-element.40), calls=%async_computation.1 | async-start | bytes 2097152 | tf_op jit(solution)/shard_map/all_to_all | solution.py:691
  168.0 15.6 %collective-permute-start.13 = (bf16[2048,512]{0,1:T(8,128)(2,1)}, bf16[2048,512]{0,1:T(8,128)(2,1)}, u32[]{:S(2)}, u32[]{:S(2)}) collective-permute-start(bf16[2048,512]{0,1:T(8,128)(2,1)} %convolution_convert_fusion.3), channel_id=1, source_target_pairs={{0,2},{2,0},{4,6},{6,4},{8,10},{10,8},{12,14},{14,12},{16,18},{18,... | collective-permute-start | bytes 6291464 | tf_op jit(solution)/shard_map/ppermute | solution.py:544
  171.6 49.0 %collective-permute-start.46 = (bf16[2048,512]{0,1:T(8,128)(2,1)}, bf16[2048,512]{0,1:T(8,128)(2,1)S(1)}, u32[]{:S(2)}, u32[]{:S(2)}) collective-permute-start(bf16[2048,512]{0,1:T(8,128)(2,1)} %convolution_convert_fusion), channel_id=1, source_target_pairs={{0,2},{2,0},{4,6},{6,4},{8,10},{10,8},{12,14},{14,12},{16,18},{18,... | collective-permute-start | bytes 6291464 | tf_op jit(solution)/shard_map/ppermute | solution.py:544
  177.0 54.1 %all-to-all-start.2 = ((bf16[16,2,128,128]{3,2,1,0:T(8,128)(2,1)}), bf16[16,2,128,128]{3,2,1,0:T(8,128)(2,1)}, u32[]{:S(2)}, u32[]{:S(2)}) async-start(bf16[16,2,128,128]{3,2,1,0:T(8,128)(2,1)} %get-tuple-element.51), calls=%async_computation.2 | async-start | bytes 2097152 | tf_op jit(solution)/shard_map/all_to_all | solution.py:698
  190.2 48.3 %collective-permute-start.14 = (bf16[2048,256]{0,1:T(8,128)(2,1)}, bf16[2048,256]{0,1:T(8,128)(2,1)}, u32[]{:S(2)}, u32[]{:S(2)}) collective-permute-start(bf16[2048,256]{0,1:T(8,128)(2,1)} %slice.464), channel_id=1, source_target_pairs={{0,1},{1,0},{2,3},{3,2},{4,5},{5,4},{6,7},{7,6},{8,9},{9,8},{10,11... | collective-permute-start | bytes 3145736 | tf_op jit(solution)/shard_map/ppermute | solution.py:544
  226.6 32.8 %collective-permute-start.47 = (bf16[2048,256]{0,1:T(8,128)(2,1)}, bf16[2048,256]{0,1:T(8,128)(2,1)S(1)}, u32[]{:S(2)}, u32[]{:S(2)}) collective-permute-start(bf16[2048,256]{0,1:T(8,128)(2,1)} %slice.463), channel_id=1, source_target_pairs={{0,4},{2,6},{4,0},{6,2},{8,12},{10,14},{12,8},{14,10},{16,20},{18,... | collective-permute-start | bytes 3145736 | tf_op jit(solution)/shard_map/ppermute | solution.py:544
  233.6 76.1 %all-to-all-start.3 = ((bf16[16,2,128,128]{3,2,1,0:T(8,128)(2,1)}), bf16[16,2,128,128]{3,2,1,0:T(8,128)(2,1)S(1)}, u32[]{:S(2)}, u32[]{:S(2)}) async-start(bf16[16,2,128,128]{3,2,1,0:T(8,128)(2,1)} %shard_map.199), calls=%async_computation.3 | async-start | bytes 2097152 | tf_op jit(solution)/shard_map/all_to_all | solution.py:701
  240.9 33.5 %collective-permute-start.15 = (bf16[2048,128]{0,1:T(8,128)(2,1)S(1)}, bf16[2048,128]{0,1:T(8,128)(2,1)S(1)}, u32[]{:S(2)}, u32[]{:S(2)}) collective-permute-start(bf16[2048,128]{0,1:T(8,128)(2,1)S(1)} %slice.468), channel_id=1, source_target_pairs={{0,4},{2,6},{4,0},{6,2},{8,12},{10,14},{12,8},{14,10},{16,20},{18,... | collective-permute-start | bytes 1572872 | tf_op jit(solution)/shard_map/ppermute | solution.py:544
  259.8 19.4 %collective-permute-start.48 = (bf16[1024,256]{0,1:T(8,128)(2,1)S(1)}, bf16[1024,256]{0,1:T(8,128)(2,1)S(1)}, u32[]{:S(2)}, u32[]{:S(2)}) collective-permute-start(bf16[1024,256]{0,1:T(8,128)(2,1)S(1)} %slice.467), channel_id=1, source_target_pairs={{0,1},{1,0},{2,3},{3,2},{4,5},{5,4},{6,7},{7,6},{8,9},{9,8},{10,11... | collective-permute-start | bytes 1572872 | tf_op jit(solution)/shard_map/ppermute | solution.py:544
  274.6 8.8 %collective-permute-start.18 = (bf16[512,128]{0,1:T(8,128)(2,1)S(1)}, bf16[512,128]{0,1:T(8,128)(2,1)S(1)}, u32[]{:S(2)}, u32[]{:S(2)}) collective-permute-start(bf16[512,128]{0,1:T(8,128)(2,1)S(1)} %get-tuple-element.101), channel_id=1, source_target_pairs={{0,24},{2,26},{4,28},{6,30},{8,0},{10,2},{12,4},{14,6},{16,8},{18,... | collective-permute-start | bytes 393224 | tf_op jit(solution)/shard_map/ppermute | solution.py:606
  278.1 19.0 %collective-permute-start.17 = (bf16[512,128]{0,1:T(8,128)(2,1)S(1)}, bf16[512,128]{0,1:T(8,128)(2,1)S(1)}, u32[]{:S(2)}, u32[]{:S(2)}) collective-permute-start(bf16[512,128]{0,1:T(8,128)(2,1)S(1)} %get-tuple-element.102), channel_id=1, source_target_pairs={{0,16},{2,18},{4,20},{6,22},{8,24},{10,26},{12,28},{14,30},{16,0},... | collective-permute-start | bytes 393224 | tf_op jit(solution)/shard_map/ppermute | solution.py:606
  278.1 19.0 %collective-permute-start.16 = (bf16[512,128]{0,1:T(8,128)(2,1)S(1)}, bf16[512,128]{0,1:T(8,128)(2,1)S(1)}, u32[]{:S(2)}, u32[]{:S(2)}) collective-permute-start(bf16[512,128]{0,1:T(8,128)(2,1)S(1)} %get-tuple-element.100), channel_id=1, source_target_pairs={{0,8},{2,10},{4,12},{6,14},{8,16},{10,18},{12,20},{14,22},{16,24},... | collective-permute-start | bytes 393224 | tf_op jit(solution)/shard_map/ppermute | solution.py:606
  279.5 20.1 %collective-permute-start.51 = (bf16[256,256]{0,1:T(8,128)(2,1)S(1)}, bf16[256,256]{0,1:T(8,128)(2,1)S(1)}, u32[]{:S(2)}, u32[]{:S(2)}) collective-permute-start(bf16[256,256]{0,1:T(8,128)(2,1)S(1)} %get-tuple-element.96), channel_id=1, source_target_pairs={{0,24},{2,26},{4,28},{6,30},{8,0},{10,2},{12,4},{14,6},{16,8},{18,... | collective-permute-start | bytes 393224 | tf_op jit(solution)/shard_map/ppermute | solution.py:606
  282.2 21.9 %collective-permute-start.50 = (bf16[256,256]{0,1:T(8,128)(2,1)S(1)}, bf16[256,256]{0,1:T(8,128)(2,1)S(1)}, u32[]{:S(2)}, u32[]{:S(2)}) collective-permute-start(bf16[256,256]{0,1:T(8,128)(2,1)S(1)} %get-tuple-element.97), channel_id=1, source_target_pairs={{0,16},{2,18},{4,20},{6,22},{8,24},{10,26},{12,28},{14,30},{16,0},... | collective-permute-start | bytes 393224 | tf_op jit(solution)/shard_map/ppermute | solution.py:606
  283.4 20.8 %collective-permute-start.49 = (bf16[256,256]{0,1:T(8,128)(2,1)S(1)}, bf16[256,256]{0,1:T(8,128)(2,1)S(1)}, u32[]{:S(2)}, u32[]{:S(2)}) collective-permute-start(bf16[256,256]{0,1:T(8,128)(2,1)S(1)} %get-tuple-element.95), channel_id=1, source_target_pairs={{0,8},{2,10},{4,12},{6,14},{8,16},{10,18},{12,20},{14,22},{16,24},... | collective-permute-start | bytes 393224 | tf_op jit(solution)/shard_map/ppermute | solution.py:606
  298.9 40.0 %collective-permute-start.19 = (bf16[512,128]{0,1:T(8,128)(2,1)}, bf16[512,128]{0,1:T(8,128)(2,1)}, u32[]{:S(2)}, u32[]{:S(2)}) collective-permute-start(bf16[512,128]{0,1:T(8,128)(2,1)} %add_convert_fusion.1), channel_id=1, source_target_pairs={{0,8},{2,10},{4,12},{6,14},{8,16},{10,18},{12,20},{14,22},{16,24},... | collective-permute-start | bytes 393224 | tf_op jit(solution)/shard_map/ppermute | solution.py:606
  299.0 46.7 %collective-permute-start.20 = (bf16[512,128]{0,1:T(8,128)(2,1)}, bf16[512,128]{0,1:T(8,128)(2,1)}, u32[]{:S(2)}, u32[]{:S(2)}) collective-permute-start(bf16[512,128]{0,1:T(8,128)(2,1)} %add_convert_fusion.1), channel_id=1, source_target_pairs={{0,16},{2,18},{4,20},{6,22},{8,24},{10,26},{12,28},{14,30},{16,0},... | collective-permute-start | bytes 393224 | tf_op jit(solution)/shard_map/ppermute | solution.py:606
  299.6 50.8 %collective-permute-start.21 = (bf16[512,128]{0,1:T(8,128)(2,1)}, bf16[512,128]{0,1:T(8,128)(2,1)}, u32[]{:S(2)}, u32[]{:S(2)}) collective-permute-start(bf16[512,128]{0,1:T(8,128)(2,1)} %add_convert_fusion.1), channel_id=1, source_target_pairs={{0,24},{2,26},{4,28},{6,30},{8,0},{10,2},{12,4},{14,6},{16,8},{18,... | collective-permute-start | bytes 393224 | tf_op jit(solution)/shard_map/ppermute | solution.py:606
  305.9 56.3 %collective-permute-start.52 = (bf16[256,256]{0,1:T(8,128)(2,1)}, bf16[256,256]{0,1:T(8,128)(2,1)}, u32[]{:S(2)}, u32[]{:S(2)}) collective-permute-start(bf16[256,256]{0,1:T(8,128)(2,1)} %add_convert_fusion), channel_id=1, source_target_pairs={{0,8},{2,10},{4,12},{6,14},{8,16},{10,18},{12,20},{14,22},{16,24},... | collective-permute-start | bytes 393224 | tf_op jit(solution)/shard_map/ppermute | solution.py:606
  306.0 59.5 %collective-permute-start.53 = (bf16[256,256]{0,1:T(8,128)(2,1)}, bf16[256,256]{0,1:T(8,128)(2,1)}, u32[]{:S(2)}, u32[]{:S(2)}) collective-permute-start(bf16[256,256]{0,1:T(8,128)(2,1)} %add_convert_fusion), channel_id=1, source_target_pairs={{0,16},{2,18},{4,20},{6,22},{8,24},{10,26},{12,28},{14,30},{16,0},... | collective-permute-start | bytes 393224 | tf_op jit(solution)/shard_map/ppermute | solution.py:606
  338.9 28.3 %collective-permute-start.54 = (bf16[256,256]{0,1:T(8,128)(2,1)}, bf16[256,256]{0,1:T(8,128)(2,1)}, u32[]{:S(2)}, u32[]{:S(2)}) collective-permute-start(bf16[256,256]{0,1:T(8,128)(2,1)} %add_convert_fusion), channel_id=1, source_target_pairs={{0,24},{2,26},{4,28},{6,30},{8,0},{10,2},{12,4},{14,6},{16,8},{18,... | collective-permute-start | bytes 393224 | tf_op jit(solution)/shard_map/ppermute | solution.py:606
  345.6 24.7 %collective-permute-start.7 = (f32[2,8,2304]{2,1,0:T(8,128)}, f32[2,8,2304]{2,1,0:T(8,128)}, u32[]{:S(2)}, u32[]{:S(2)}) collective-permute-start(f32[2,8,2304]{2,1,0:T(8,128)} %slice.228), channel_id=1, source_target_pairs={{2,0},{4,2},{6,4},{8,6},{10,8},{12,10},{14,12},{16,14},{18,16},{20... | collective-permute-start | bytes 442376 | tf_op jit(solution)/shard_map/ppermute | solution.py:745
  360.1 59.3 %collective-permute-start.22 = (bf16[2048,128]{1,0:T(8,128)(2,1)}, bf16[2048,128]{1,0:T(8,128)(2,1)}, u32[]{:S(2)}, u32[]{:S(2)}) collective-permute-start(bf16[2048,128]{1,0:T(8,128)(2,1)} %constant_dynamic-update-slice_fusion.12), channel_id=1, source_target_pairs={{0,4},{2,6},{4,0},{6,2},{8,12},{10,14},{12,8},{14,10},{16,20},{18,... | collective-permute-start | bytes 1572872 | tf_op jit(solution)/shard_map/ppermute | solution.py:544
  385.8 1.5 collective-permute-start.8
  386.7 34.0 %collective-permute-start.55 = (bf16[1024,256]{1,0:T(8,128)(2,1)}, bf16[1024,256]{1,0:T(8,128)(2,1)}, u32[]{:S(2)}, u32[]{:S(2)}) collective-permute-start(bf16[1024,256]{1,0:T(8,128)(2,1)} %constant_dynamic-update-slice_fusion), channel_id=1, source_target_pairs={{0,4},{2,6},{4,0},{6,2},{8,12},{10,14},{12,8},{14,10},{16,20},{18,... | collective-permute-start | bytes 1572872 | tf_op jit(solution)/shard_map/ppermute | solution.py:544
  387.3 15.1 %collective-permute-start.9 = (f32[14688]{0:T(1024)S(1)}, f32[14688]{0:T(1024)S(1)}, u32[]{:S(2)}, u32[]{:S(2)}) collective-permute-start(f32[14688]{0:T(1024)S(1)} %add.324), channel_id=1, source_target_pairs={{0,4},{2,6},{4,0},{6,2},{8,12},{10,14},{12,8},{14,10},{16,20},{18,... | collective-permute-start | bytes 176264 | tf_op jit(solution)/shard_map/ppermute | solution.py:544
  402.4 4.3 collective-permute-start.10
  406.7 5.3 %collective-permute-start.11 = (f32[14688]{0:T(1024)S(1)}, f32[14688]{0:T(1024)S(1)}, u32[]{:S(2)}, u32[]{:S(2)}) collective-permute-start(f32[14688]{0:T(1024)S(1)} %add.326), channel_id=1, source_target_pairs={{0,16},{2,18},{4,20},{6,22},{8,24},{10,26},{12,28},{14,30},{16,0},... | collective-permute-start | bytes 176264 | tf_op jit(solution)/shard_map/ppermute | solution.py:544
  407.8 17.7 %collective-permute-start.35 = (bf16[1184,512]{1,0:T(8,128)(2,1)}, bf16[1184,512]{1,0:T(8,128)(2,1)}, u32[]{:S(2)}, u32[]{:S(2)}) collective-permute-start(bf16[1184,512]{1,0:T(8,128)(2,1)} %convolution_convert_fusion.1), channel_id=1, source_target_pairs={{0,2},{2,0},{4,6},{6,4},{8,10},{10,8},{12,14},{14,12},{16,18},{18,... | collective-permute-start | bytes 3637256 | tf_op jit(solution)/shard_map/ppermute | solution.py:544
  407.8 14.9 %collective-permute-start.24 = (bf16[1152,512]{1,0:T(8,128)(2,1)}, bf16[1152,512]{1,0:T(8,128)(2,1)}, u32[]{:S(2)}, u32[]{:S(2)}) collective-permute-start(bf16[1152,512]{1,0:T(8,128)(2,1)} %convolution_convert_fusion.2), channel_id=1, source_target_pairs={{0,2},{2,0},{4,6},{6,4},{8,10},{10,8},{12,14},{14,12},{16,18},{18,... | collective-permute-start | bytes 3538952 | tf_op jit(solution)/shard_map/ppermute | solution.py:544
  412.0 4.3 collective-permute-start.12
  420.7 7.4 %collective-permute-start.23 = (bf16[2048,256]{1,0:T(8,128)(2,1)S(1)}, bf16[2048,256]{1,0:T(8,128)(2,1)S(1)}, u32[]{:S(2)}, u32[]{:S(2)}) collective-permute-start(bf16[2048,256]{1,0:T(8,128)(2,1)S(1)} %pad_maximum_fusion.15), channel_id=1, source_target_pairs={{0,2},{2,0},{4,6},{6,4},{8,10},{10,8},{12,14},{14,12},{16,18},{18,... | collective-permute-start | bytes 3145736 | tf_op jit(solution)/shard_map/ppermute | solution.py:544
  422.2 6.3 %collective-permute-start.56 = (bf16[1024,512]{1,0:T(8,128)(2,1)S(1)}, bf16[1024,512]{1,0:T(8,128)(2,1)S(1)}, u32[]{:S(2)}, u32[]{:S(2)}) collective-permute-start(bf16[1024,512]{1,0:T(8,128)(2,1)S(1)} %pad_maximum_fusion.16), channel_id=1, source_target_pairs={{0,2},{2,0},{4,6},{6,4},{8,10},{10,8},{12,14},{14,12},{16,18},{18,... | collective-permute-start | bytes 3145736 | tf_op jit(solution)/shard_map/ppermute | solution.py:544
  424.9 15.4 %collective-permute-start.25 = (bf16[1152,256]{1,0:T(8,128)(2,1)S(1)}, bf16[1152,256]{1,0:T(8,128)(2,1)S(1)}, u32[]{:S(2)}, u32[]{:S(2)}) collective-permute-start(bf16[1152,256]{1,0:T(8,128)(2,1)S(1)} %slice.466), channel_id=1, source_target_pairs={{0,1},{1,0},{2,3},{3,2},{4,5},{5,4},{6,7},{7,6},{8,9},{9,8},{10,11... | collective-permute-start | bytes 1769480 | tf_op jit(solution)/shard_map/ppermute | solution.py:544
  427.7 16.1 %collective-permute-start.36 = (bf16[1184,256]{1,0:T(8,128)(2,1)S(1)}, bf16[1184,256]{1,0:T(8,128)(2,1)S(1)}, u32[]{:S(2)}, u32[]{:S(2)}) collective-permute-start(bf16[1184,256]{1,0:T(8,128)(2,1)S(1)} %slice.465), channel_id=1, source_target_pairs={{0,4},{2,6},{4,0},{6,2},{8,12},{10,14},{12,8},{14,10},{16,20},{18,... | collective-permute-start | bytes 1818632 | tf_op jit(solution)/shard_map/ppermute | solution.py:544
  440.5 8.9 %collective-permute-start.26 = (bf16[1152,128]{1,0:T(8,128)(2,1)S(1)}, bf16[1152,128]{1,0:T(8,128)(2,1)S(1)}, u32[]{:S(2)}, u32[]{:S(2)}) collective-permute-start(bf16[1152,128]{1,0:T(8,128)(2,1)S(1)} %slice.470), channel_id=1, source_target_pairs={{0,4},{2,6},{4,0},{6,2},{8,12},{10,14},{12,8},{14,10},{16,20},{18,... | collective-permute-start | bytes 884744 | tf_op jit(solution)/shard_map/ppermute | solution.py:544
  444.0 8.5 %collective-permute-start.37 = (bf16[1184,128]{1,0:T(8,128)(2,1)S(1)}, bf16[1184,128]{1,0:T(8,128)(2,1)S(1)}, u32[]{:S(2)}, u32[]{:S(2)}) collective-permute-start(bf16[1184,128]{1,0:T(8,128)(2,1)S(1)} %slice.469), channel_id=1, source_target_pairs={{0,1},{1,0},{2,3},{3,2},{4,5},{5,4},{6,7},{7,6},{8,9},{9,8},{10,11... | collective-permute-start | bytes 909320 | tf_op jit(solution)/shard_map/ppermute | solution.py:544
  449.6 5.5 %collective-permute-start.29 = (bf16[288,128]{1,0:T(8,128)(2,1)S(1)}, bf16[288,128]{1,0:T(8,128)(2,1)S(1)}, u32[]{:S(2)}, u32[]{:S(2)}) collective-permute-start(bf16[288,128]{1,0:T(8,128)(2,1)S(1)} %get-tuple-element.115), channel_id=1, source_target_pairs={{0,24},{2,26},{4,28},{6,30},{8,0},{10,2},{12,4},{14,6},{16,8},{18,... | collective-permute-start | bytes 221192 | tf_op jit(solution)/shard_map/ppermute | solution.py:606
  449.9 10.2 %collective-permute-start.28 = (bf16[288,128]{1,0:T(8,128)(2,1)S(1)}, bf16[288,128]{1,0:T(8,128)(2,1)S(1)}, u32[]{:S(2)}, u32[]{:S(2)}) collective-permute-start(bf16[288,128]{1,0:T(8,128)(2,1)S(1)} %get-tuple-element.116), channel_id=1, source_target_pairs={{0,16},{2,18},{4,20},{6,22},{8,24},{10,26},{12,28},{14,30},{16,0},... | collective-permute-start | bytes 221192 | tf_op jit(solution)/shard_map/ppermute | solution.py:606
  451.0 9.2 %collective-permute-start.27 = (bf16[288,128]{1,0:T(8,128)(2,1)S(1)}, bf16[288,128]{1,0:T(8,128)(2,1)S(1)}, u32[]{:S(2)}, u32[]{:S(2)}) collective-permute-start(bf16[288,128]{1,0:T(8,128)(2,1)S(1)} %get-tuple-element.114), channel_id=1, source_target_pairs={{0,8},{2,10},{4,12},{6,14},{8,16},{10,18},{12,20},{14,22},{16,24},... | collective-permute-start | bytes 221192 | tf_op jit(solution)/shard_map/ppermute | solution.py:606
  452.7 10.6 %collective-permute-start.40 = (bf16[296,128]{1,0:T(8,128)(2,1)S(1)}, bf16[296,128]{1,0:T(8,128)(2,1)S(1)}, u32[]{:S(2)}, u32[]{:S(2)}) collective-permute-start(bf16[296,128]{1,0:T(8,128)(2,1)S(1)} %get-tuple-element.110), channel_id=1, source_target_pairs={{0,24},{2,26},{4,28},{6,30},{8,0},{10,2},{12,4},{14,6},{16,8},{18,... | collective-permute-start | bytes 227336 | tf_op jit(solution)/shard_map/ppermute | solution.py:606
  455.0 12.7 %collective-permute-start.39 = (bf16[296,128]{1,0:T(8,128)(2,1)S(1)}, bf16[296,128]{1,0:T(8,128)(2,1)S(1)}, u32[]{:S(2)}, u32[]{:S(2)}) collective-permute-start(bf16[296,128]{1,0:T(8,128)(2,1)S(1)} %get-tuple-element.111), channel_id=1, source_target_pairs={{0,16},{2,18},{4,20},{6,22},{8,24},{10,26},{12,28},{14,30},{16,0},... | collective-permute-start | bytes 227336 | tf_op jit(solution)/shard_map/ppermute | solution.py:606
  455.1 12.6 %collective-permute-start.38 = (bf16[296,128]{1,0:T(8,128)(2,1)S(1)}, bf16[296,128]{1,0:T(8,128)(2,1)S(1)}, u32[]{:S(2)}, u32[]{:S(2)}) collective-permute-start(bf16[296,128]{1,0:T(8,128)(2,1)S(1)} %get-tuple-element.109), channel_id=1, source_target_pairs={{0,8},{2,10},{4,12},{6,14},{8,16},{10,18},{12,20},{14,22},{16,24},... | collective-permute-start | bytes 227336 | tf_op jit(solution)/shard_map/ppermute | solution.py:606
  460.3 8.6 %collective-permute-start.30 = (bf16[288,128]{1,0:T(8,128)(2,1)S(1)}, bf16[288,128]{1,0:T(8,128)(2,1)S(1)}, u32[]{:S(2)}, u32[]{:S(2)}) collective-permute-start(bf16[288,128]{1,0:T(8,128)(2,1)S(1)} %get-tuple-element.68), channel_id=1, source_target_pairs={{0,8},{2,10},{4,12},{6,14},{8,16},{10,18},{12,20},{14,22},{16,24},... | collective-permute-start | bytes 221192 | tf_op jit(solution)/shard_map/ppermute | solution.py:606
  461.1 10.6 %collective-permute-start.31 = (bf16[288,128]{1,0:T(8,128)(2,1)S(1)}, bf16[288,128]{1,0:T(8,128)(2,1)S(1)}, u32[]{:S(2)}, u32[]{:S(2)}) collective-permute-start(bf16[288,128]{1,0:T(8,128)(2,1)S(1)} %get-tuple-element.68), channel_id=1, source_target_pairs={{0,16},{2,18},{4,20},{6,22},{8,24},{10,26},{12,28},{14,30},{16,0},... | collective-permute-start | bytes 221192 | tf_op jit(solution)/shard_map/ppermute | solution.py:606
  463.2 8.5 %collective-permute-start.32 = (bf16[288,128]{1,0:T(8,128)(2,1)S(1)}, bf16[288,128]{1,0:T(8,128)(2,1)S(1)}, u32[]{:S(2)}, u32[]{:S(2)}) collective-permute-start(bf16[288,128]{1,0:T(8,128)(2,1)S(1)} %get-tuple-element.68), channel_id=1, source_target_pairs={{0,24},{2,26},{4,28},{6,30},{8,0},{10,2},{12,4},{14,6},{16,8},{18,... | collective-permute-start | bytes 221192 | tf_op jit(solution)/shard_map/ppermute | solution.py:606
  467.8 6.4 %collective-permute-start.41 = (bf16[296,128]{1,0:T(8,128)(2,1)S(1)}, bf16[296,128]{1,0:T(8,128)(2,1)S(1)}, u32[]{:S(2)}, u32[]{:S(2)}) collective-permute-start(bf16[296,128]{1,0:T(8,128)(2,1)S(1)} %get-tuple-element.70), channel_id=1, source_target_pairs={{0,8},{2,10},{4,12},{6,14},{8,16},{10,18},{12,20},{14,22},{16,24},... | collective-permute-start | bytes 227336 | tf_op jit(solution)/shard_map/ppermute | solution.py:606
  467.8 8.4 %collective-permute-start.42 = (bf16[296,128]{1,0:T(8,128)(2,1)S(1)}, bf16[296,128]{1,0:T(8,128)(2,1)S(1)}, u32[]{:S(2)}, u32[]{:S(2)}) collective-permute-start(bf16[296,128]{1,0:T(8,128)(2,1)S(1)} %get-tuple-element.70), channel_id=1, source_target_pairs={{0,16},{2,18},{4,20},{6,22},{8,24},{10,26},{12,28},{14,30},{16,0},... | collective-permute-start | bytes 227336 | tf_op jit(solution)/shard_map/ppermute | solution.py:606
  468.8 7.4 %collective-permute-start.43 = (bf16[296,128]{1,0:T(8,128)(2,1)S(1)}, bf16[296,128]{1,0:T(8,128)(2,1)S(1)}, u32[]{:S(2)}, u32[]{:S(2)}) collective-permute-start(bf16[296,128]{1,0:T(8,128)(2,1)S(1)} %get-tuple-element.70), channel_id=1, source_target_pairs={{0,24},{2,26},{4,28},{6,30},{8,0},{10,2},{12,4},{14,6},{16,8},{18,... | collective-permute-start | bytes 227336 | tf_op jit(solution)/shard_map/ppermute | solution.py:606
  471.8 9.9 %collective-permute-start.33 = (bf16[1152,128]{1,0:T(8,128)(2,1)S(1)}, bf16[1152,128]{1,0:T(8,128)(2,1)S(1)}, u32[]{:S(2)}, u32[]{:S(2)}) collective-permute-start(bf16[1152,128]{1,0:T(8,128)(2,1)S(1)} %constant_dynamic-update-slice_fusion.8), channel_id=1, source_target_pairs={{0,4},{2,6},{4,0},{6,2},{8,12},{10,14},{12,8},{14,10},{16,20},{18,... | collective-permute-start | bytes 884744 | tf_op jit(solution)/shard_map/ppermute | solution.py:544
  476.3 8.7 %collective-permute-start.44 = (bf16[1184,128]{1,0:T(8,128)(2,1)S(1)}, bf16[1184,128]{1,0:T(8,128)(2,1)S(1)}, u32[]{:S(2)}, u32[]{:S(2)}) collective-permute-start(bf16[1184,128]{1,0:T(8,128)(2,1)S(1)} %constant_dynamic-update-slice_fusion.4), channel_id=1, source_target_pairs={{0,4},{2,6},{4,0},{6,2},{8,12},{10,14},{12,8},{14,10},{16,20},{18,... | collective-permute-start | bytes 909320 | tf_op jit(solution)/shard_map/ppermute | solution.py:544
  481.8 5.9 %collective-permute-start.34 = (bf16[1152,256]{1,0:T(8,128)(2,1)S(1)}, bf16[1152,256]{1,0:T(8,128)(2,1)S(1)}, u32[]{:S(2)}, u32[]{:S(2)}) collective-permute-start(bf16[1152,256]{1,0:T(8,128)(2,1)S(1)} %pad_maximum_fusion.23), channel_id=1, source_target_pairs={{0,2},{2,0},{4,6},{6,4},{8,10},{10,8},{12,14},{14,12},{16,18},{18,... | collective-permute-start | bytes 1769480 | tf_op jit(solution)/shard_map/ppermute | solution.py:544
  485.1 2.9 collective-permute-start.45
  (69 other events, 583.4 us)

commit v2 on v1

--- a/solution.py
+++ b/solution.py
@@ -33,9 +33,41 @@
     return lax.broadcasted_iota(jnp.int32, shape, dim)
 
 
+def split(a):
+    high = a.astype(bf16)
+    return high, (a - high.astype(f32)).astype(bf16)
+
+
+def mxu(a, b, dims):
+    return lax.dot_general(a, b, (dims, ((), ())), preferred_element_type=f32)
+
+
+def dot3(a, b, dims):
+    a_high, a_low = split(a)
+    b_high, b_low = split(b)
+    return mxu(a_high, b_high, dims) + (mxu(a_high, b_low, dims) + mxu(a_low, b_high, dims))
+
+
+def dot2(a, b, dims):
+    a_high, a_low = split(a)
+    return mxu(a_high, b, dims) + mxu(a_low, b, dims)
+
+
 def spread_matrix(heads):
     shape = (heads, heads * HEADDIM)
-    return (iota(shape, 1) // HEADDIM == iota(shape, 0)).astype(f32)
+    return (iota(shape, 1) // HEADDIM == iota(shape, 0)).astype(f32).astype(bf16)
+
+
+def widen(a, spread):
+    high, low = split(a)
+    return mxu(jnp.concatenate([high, low], axis=1), jnp.concatenate([spread, spread], axis=0), NN)
+
+
+def widen_row(a, spread):
+    high, low = split(jnp.broadcast_to(a, (16, a.shape[1])))
+    rest = a - high[0:1].astype(f32) - low[0:1].astype(f32)
+    rest = jnp.broadcast_to(rest, (16, a.shape[1])).astype(bf16)
+    return (mxu(high, spread, NN) + (mxu(low, spread, NN) + mxu(rest, spread, NN)))[0:1]
 
 
 def sigmoid(v):
@@ -87,8 +119,8 @@
     last = cum[length - 1 :, :]
     weight = jnp.exp(last - cum) * step
     spread = spread_matrix(heads)
-    weight_wide = exact(weight, spread, NN)
-    last_wide = exact(jnp.broadcast_to(last, (8, heads)), spread, NN)[0:1]
+    weight_wide = widen(weight, spread)
+    last_wide = widen_row(last, spread)
     write_side = None
     for start in list(range(inner, channels, 128)) + list(range(0, inner, 128)):
         cols = slice(start, start + 128)
@@ -102,7 +134,7 @@
             write_side = total * sigmoid(total)
         elif start < inner:
             xw_ref[:, cols] = total * sigmoid(total) * weight_wide[:, cols]
-    state = exact(write_side, xw_ref[...], TN)
+    state = dot3(write_side, xw_ref[...], TN)
     width = send_ref.shape[3]
     hi = last_wide.astype(bf16)
     rest = last_wide - hi.astype(f32)
@@ -214,21 +246,28 @@
     inner = heads * HEADDIM
     write_conv = conv_ref[0, :, inner : inner + STATE]
     read_conv = conv_ref[0, :, inner + STATE :]
-    products = exact(read_conv * sigmoid(read_conv), write_conv * sigmoid(write_conv), NT)
+    products = dot3(read_conv * sigmoid(read_conv), write_conv * sigmoid(write_conv), NT)
     cum = cum_ref[0]
     cum_t = columns(cum)
-    dt_wide = exact(dt_ref[0], spread_matrix(heads), NN)
+    dt_wide = widen(dt_ref[0], spread_matrix(heads))
     causal = iota((length, length), 0) >= iota((length, length), 1)
     left = iota((length, 2 * HEADDIM), 1) < HEADDIM
     for pair in range(heads // 2):
         cols = slice(pair * 2 * HEADDIM, (pair + 1) * 2 * HEADDIM)
         conv = conv_ref[0, :, cols]
         scaled = conv * sigmoid(conv) * dt_wide[:, cols]
-        parts = []
+        terms = []
         for head in (2 * pair, 2 * pair + 1):
             gap = cum[:, head : head + 1] - cum_t[head : head + 1, :]
-            weights = jnp.exp(jnp.where(causal, gap, -1e30)) * products
-            parts.append(exact(weights, scaled, NN))
+            terms += split(jnp.exp(jnp.where(causal, gap, -1e30)) * products)
+        every = mxu(
+            jnp.concatenate(terms, axis=0), jnp.concatenate(split(scaled), axis=1), NN
+        )
+        high, low = every[:, : 2 * HEADDIM], every[:, 2 * HEADDIM :]
+        parts = [
+            high[at : at + length] + (low[at : at + length] + high[at + length : at + 2 * length])
+            for at in (0, 2 * length)
+        ]
         y_ref[0, :, cols] = jnp.where(left, parts[0], parts[1])
 
 
@@ -257,14 +296,14 @@
     inner = heads * HEADDIM
     dests, _, _, width = start_ref.shape
     for dest in range(dests):
-        state_ref[:, dest * width : (dest + 1) * width] = start_ref[dest, 0].astype(f32)
+        state_ref[:, dest * width : (dest + 1) * width] = start_ref[dest, 0]
     read_conv = conv_ref[0, :, inner + STATE :]
     read_side = read_conv * sigmoid(read_conv)
     spread = spread_matrix(heads)
     grow = jnp.exp(cum_ref[0])
-    grow_wide = exact(grow, spread, NN)
-    skip_wide = exact(jnp.broadcast_to(skip_ref[...], (8, heads)), spread, NN)[0:1]
-    scan_ref[...] = exact(read_side, state_ref[...], NN) * grow_wide + y_ref[0]
+    grow_wide = widen(grow, spread)
+    skip_wide = widen_row(skip_ref[...], spread)
+    scan_ref[...] = dot2(read_side, state_ref[...], NN) * grow_wide + y_ref[0]
     square = jnp.zeros((length, 128), f32)
     for start in range(0, inner, 128):
         cols = slice(start, start + 128)
@@ -303,9 +342,9 @@
         scan_ref[:, cols] = scanned * grad_mixed
         skip_part_ref[0, :, cols] = jnp.sum(values * grad_mixed, axis=0, keepdims=True)
         gated_ref[:, cols] = grad_mixed * grow_wide[:, cols]
-    gs_ref[0] = exact(scan_ref[...], spread, NT)
-    cread_ref[0] = exact(gated_ref[...], state_ref[...], NT)
-    back = exact(read_side, gated_ref[...], TN)
+    gs_ref[0] = dot2(scan_ref[...], spread, NT)
+    cread_ref[0] = dot2(gated_ref[...], state_ref[...], NT)
+    back = dot3(read_side, gated_ref[...], TN)
     for dest in range(dests):
         send_ref[dest, 0] = back[:, dest * width : (dest + 1) * width].astype(send_ref.dtype)
 
@@ -349,11 +388,11 @@
             jax.ShapeDtypeStruct((seqs, length, STATE), f32),
         ],
         [
-            pltpu.VMEM((STATE, inner), f32),
+            pltpu.VMEM((STATE, inner), start.dtype),
             pltpu.VMEM((length, inner), f32),
             pltpu.VMEM((length, inner), f32),
         ],
-        flops=36 * seqs * length * STATE * inner,
+        flops=12 * seqs * length * STATE * inner,
         moved=seqs * length * channels * 20,
     )(y, conv, cum, start, gate, gate_gain[None], skip_gain[None], grad_normed)
 
@@ -366,10 +405,10 @@
     read_conv = conv_ref[0, :, inner + STATE :]
     write_side = write_conv * sigmoid(write_conv)
     read_side = read_conv * sigmoid(read_conv)
-    products = exact(write_side, read_side, NT)
+    products = dot3(write_side, read_side, NT)
     cum = cum_ref[0]
     cum_t = columns(cum)
-    dt_wide = exact(dt_ref[0], spread_matrix(heads), NN)
+    dt_wide = widen(dt_ref[0], spread_matrix(heads))
     causal = iota((length, length), 0) <= iota((length, length), 1)
     left = iota((length, 2 * HEADDIM), 1) < HEADDIM
     grad_products = jnp.zeros((length, length), f32)
@@ -377,17 +416,23 @@
         cols = slice(pair * 2 * HEADDIM, (pair + 1) * 2 * HEADDIM)
         conv = conv_ref[0, :, cols]
         scaled = conv * sigmoid(conv) * dt_wide[:, cols]
-        grad = gm_ref[0, :, cols].astype(f32)
-        parts = []
+        grad = gm_ref[0, :, cols]
+        terms, own, decays = [], [], []
         for side, head in enumerate((2 * pair, 2 * pair + 1)):
             gap = cum_t[head : head + 1, :] - cum[:, head : head + 1]
-            decays = jnp.exp(jnp.where(causal, gap, -1e30))
-            parts.append(exact(decays * products, grad, NN))
-            own = jnp.where(left if side == 0 else ~left, scaled, 0.0)
-            grad_products = grad_products + decays * exact(own, grad, NT)
+            decays.append(jnp.exp(jnp.where(causal, gap, -1e30)))
+            terms += split(decays[side] * products)
+            own += split(jnp.where(left if side == 0 else ~left, scaled, 0.0))
+        every = mxu(jnp.concatenate(terms, axis=0), grad, NN)
+        cross = mxu(jnp.concatenate(own, axis=0), grad, NT)
+        parts = []
+        for side, at in enumerate((0, 2 * length)):
+            parts.append(every[at : at + length] + every[at + length : at + 2 * length])
+            cross_head = cross[at : at + length] + cross[at + length : at + 2 * length]
+            grad_products = grad_products + decays[side] * cross_head
         u_ref[0, :, cols] = jnp.where(left, parts[0], parts[1])
-    dw_ref[0] = exact(grad_products, read_side, NN)
-    dr_ref[0] = exact(grad_products, write_side, TN) + cread_ref[0]
+    dw_ref[0] = dot3(grad_products, read_side, NN)
+    dr_ref[0] = dot3(grad_products, write_side, TN) + cread_ref[0]
 
 
 def scan_within_back(conv, dt, cum, grad_mixed, cread):
@@ -432,19 +477,19 @@
     cum = cum_ref[0]
     last = cum[length - 1 :, :]
     weight = jnp.exp(last - cum)
-    step_wide = exact(step, spread, NN)
-    weight_wide = exact(weight, spread, NN)
-    skip_wide = exact(jnp.broadcast_to(skip_ref[...], (8, heads)), spread, NN)[0:1]
+    step_wide = widen(step, spread)
+    weight_wide = widen(weight, spread)
+    skip_wide = widen_row(skip_ref[...], spread)
     inner_sum = []
     for dest in range(dests):
         cols = slice(dest * width, (dest + 1) * width)
+        state_ref[:, cols] = end_ref[dest, 0]
         end = end_ref[dest, 0].astype(f32)
-        state_ref[:, cols] = end
         inner_sum.append(jnp.sum(end * start_ref[dest, 0].astype(f32), axis=0, keepdims=True))
     inner_sum = jnp.concatenate(inner_sum, axis=1)
     write_conv = conv_ref[0, :, inner : inner + STATE]
     write_side = write_conv * sigmoid(write_conv)
-    xs_ref[...] = exact(write_side, state_ref[...], NN) * weight_wide
+    xs_ref[...] = dot2(write_side, state_ref[...], NN) * weight_wide
 
     def conv_back(start, grad):
         cols = slice(start, start + 128)
@@ -471,11 +516,11 @@
         xw_ref[:, cols] = values * (step_wide[:, cols] * weight_wide[:, cols])
         grad = step_wide[:, cols] * total + skip_wide[:, cols] * gm_ref[0, :, cols].astype(f32)
         conv_back(start, grad)
-    conv_back(inner, dw_ref[0] + exact(xw_ref[...], state_ref[...], NT))
+    conv_back(inner, dw_ref[0] + dot2(xw_ref[...], state_ref[...], NT))
     conv_back(inner + STATE, dr_ref[0])
-    direct = exact(xu_ref[...], spread, NT)
-    ends = exact(xs_ref[...], spread, NT) * step
-    held = exact(jnp.broadcast_to(inner_sum, (8, inner)), spread, NT)[0:1] * jnp.exp(last)
+    direct = dot2(xu_ref[...], spread, NT)
+    ends = dot2(xs_ref[...], spread, NT) * step
+    held = dot2(jnp.broadcast_to(inner_sum, (16, inner)), spread, NT)[0:1] * jnp.exp(last)
     at_end = jnp.sum(ends, axis=0, keepdims=True) + held
     dcum = gs_ref[0] - step * direct
     dcum = dcum + jnp.where(iota((length, heads), 0) == length - 1, at_end, 0.0)
@@ -528,12 +573,12 @@
             jax.ShapeDtypeStruct((seqs, 1, heads), f32),
         ],
         [
-            pltpu.VMEM((STATE, inner), f32),
+            pltpu.VMEM((STATE, inner), end.dtype),
             pltpu.VMEM((length, inner), f32),
             pltpu.VMEM((length, inner), f32),
             pltpu.VMEM((length, inner), f32),
         ],
-        flops=24 * seqs * length * STATE * inner,
+        flops=10 * seqs * length * STATE * inner,
         moved=seqs * length * channels * 24,
     )(u, dw, dr, conv, p_ext, dt, cum, gm, gs, start, end, conv_weight,
       dt_bias[None], a_log[None], skip_gain[None])
@@ -575,18 +620,20 @@
     return jnp.concatenate([low, high], axis=axis)
 
 
-def fetch_rows(w):
+def fetch_rows(w, after=None):
     _, _, odd, _ = shared_slots()
     mine, _ = halves(w, odd, 0)
     fetched = swap(mine, "fsdp", 1)
+    if after is not None:
+        fetched, _ = lax.optimization_barrier((fetched, after))
     return fetched, swap(fetched, "seq", 1)
 
 
-def gather_rows(w):
+def gather_rows(w, after=None):
     if not fast_mesh():
         return lax.all_gather(w, "fsdp", axis=0, tiled=True)
     _, _, odd, second = shared_slots()
-    fetched, shared = fetch_rows(w)
+    fetched, shared = fetch_rows(w, after)
     return join(w, join(fetched, shared, odd, 0), second, 0)
 
 
@@ -615,22 +662,46 @@
     return mine
 
 
-def gather_z(mine, z):
-    size = mine.shape[0]
-    total = jnp.zeros((4 * size,) + mine.shape[1:], mine.dtype)
-    total = lax.dynamic_update_slice_in_dim(total, mine, z * size, 0)
-    for shift in range(1, 4):
-        total = lax.dynamic_update_slice_in_dim(
-            total, ring(mine, shift), (z - shift) % 4 * size, 0
-        )
-    return total
-
-
 def spread_total(mine):
-    z, x, odd, _ = shared_slots()
-    total = gather_z(mine.astype(bf16), z)
-    total = join(total, swap(total, "seq", 2), x, 1)
-    return join(total, swap(total, "seq", 1), odd, 1)
+    total = mine.astype(bf16)
+    total = jnp.concatenate([total] + [ring(total, shift) for shift in range(1, 4)], axis=0)
+    total = jnp.concatenate([total, swap(total, "seq", 2)], axis=1)
+    return total, swap(total, "seq", 1)
+
+
+def place_body(bases, slots_ref, *refs):
+    out_ref = refs[-1]
+    z, x, core = slots_ref[0], slots_ref[1], slots_ref[2]
+    for piece, base in enumerate(bases):
+        for side in range(2):
+            src = refs[2 * piece + side]
+            rows, cols = src.shape[0] // 4, src.shape[1] // 2
+            for shift in range(4):
+                row = pl.multiple_of(base + lax.rem(z + 4 - shift, 4) * rows, 8)
+                for k in range(2):
+                    at = lax.rem(core + side, 2) * 2 + lax.rem(x + k, 2)
+                    out_ref[pl.ds(row, rows), pl.ds(pl.multiple_of(at * cols, 128), cols)] = src[
+                        shift * rows : (shift + 1) * rows, k * cols : (k + 1) * cols
+                    ].astype(f32)
+
+
+def place(slots, pieces, shape):
+    bases, flat, base = [], [], 0
+    for own, other in pieces:
+        bases.append(base)
+        base += own.shape[0]
+        flat += [own, other]
+    return pl.pallas_call(
+        functools.partial(place_body, bases),
+        in_specs=[pl.BlockSpec(memory_space=pltpu.SMEM)]
+        + [pl.BlockSpec(memory_space=pltpu.VMEM)] * len(flat),
+        out_specs=pl.BlockSpec(memory_space=pltpu.VMEM),
+        out_shape=jax.ShapeDtypeStruct(shape, f32),
+        compiler_params=pltpu.CompilerParams(vmem_limit_bytes=VMEM_BYTES),
+        cost_estimate=pl.CostEstimate(
+            flops=0, bytes_accessed=6 * shape[0] * shape[1], transcendentals=0
+        ),
+    )(slots, *flat)
 
 
 def dot(a, b, dims):
@@ -653,7 +724,6 @@
     backward = [(slot + 1, slot) for slot in range(seq_count - 1)]
 
     w_gate, w_scan = in_weight[:, :inner], in_weight[:, inner:]
-    halo = lax.ppermute(hidden_in[:, length - HALO :], "seq", forward)
     fast = fast_mesh()
     if fast:
         z, x, odd, second = shared_slots()
@@ -667,6 +737,8 @@
 
     residual = hidden_in.astype(f32)
     inv_rms, scaled_low = prenorm(residual)
+    halo = lax.optimization_barrier((hidden_in, scaled_low))[0][:, length - HALO :]
+    halo = lax.ppermute(halo, "seq", forward)
     _, scaled_halo = prenorm(halo.astype(f32))
     scaled_ext = jnp.concatenate([scaled_halo, scaled_low], axis=1)
     scaled_low = scaled_low.reshape(rows, width)
@@ -683,10 +755,10 @@
         p_ext, conv_weight, conv_bias, dt_bias, a_log, seq_count, STATE_TYPE
     )
     recv = lax.all_to_all(send, "seq", split_axis=0, concat_axis=0, tiled=True)
-    w_gate, w_out, _ = lax.optimization_barrier((w_gate, out_weight, p_ext))
-    gate_full = gather_rows(w_gate)
-    out_full = gather_rows(w_out)
+    w_gate, w_out, conv = lax.optimization_barrier((w_gate, out_weight, conv))
     y = scan_within(conv, dt, cum)
+    gate_full = gather_rows(w_gate, y)
+    out_full = gather_rows(w_out, y)
     start_heads, decay = combine(recv)
     start = lax.all_to_all(start_heads, "seq", split_axis=0, concat_axis=0, tiled=True)
     gate = dot(scaled_low, gate_full, NN).astype(bf16).reshape(seqs, length, inner)
@@ -715,26 +787,23 @@
             jnp.concatenate([eighths[y][c][k] for k in (0, 1) for y in (0, 1)], axis=1)
             for c in (0, 1)
         ]
+        slots = jnp.stack([z, x.astype(jnp.int32), odd.astype(jnp.int32)]).astype(jnp.int32)
 
         def near(left, right):
             keep = dot(left, right[0], TN)
             give = dot(left, right[1], TN).astype(bf16)
             return keep + swap(give, "seq", 1).astype(f32)
 
-        def reduce_y(left):
-            total = fold(fold(near(left, by_y), "fsdp", 1, 1), "seq", 2, 1)
-            return spread_total(scatter_z(total, z))
-
-        def reduce_x(left):
-            total = fold(fold(near(left, by_x), "seq", 2, 1), "fsdp", 1, 1)
-            return spread_total(scatter_z(total, z))
-
         sides = [halves(side, x, 1) for side in halves(grad_rows, odd, 1)]
         cot = [jnp.concatenate(side, axis=1) for side in sides]
-        total = near(jnp.concatenate(halves(normed, second, 1), axis=1), cot)
-        total = fold(fold(total, "seq", 2, 1), "fsdp", 1, 0)
-        out_total = spread_total(scatter_z(total, z)).astype(f32)
-        gate_total = reduce_y(grad_gate)
+        normed_late, gate_late, _ = lax.optimization_barrier((normed, grad_gate, u))
+        total = near(jnp.concatenate(halves(normed_late, second, 1), axis=1), cot)
+        out_part = fold(total, "fsdp", 1, 0)
+        gate_part = fold(near(gate_late, by_y), "fsdp", 1, 1)
+        out_part, gate_part, end = lax.optimization_barrier((out_part, gate_part, end))
+        out_pair = spread_total(scatter_z(fold(out_part, "seq", 2, 1), z))
+        gate_pair = spread_total(scatter_z(fold(gate_part, "seq", 2, 1), z))
+        out_total = place(slots, [out_pair], out_weight.shape)
     else:
         out_total = reduce_rows(dot(normed, grad_rows, TN))
         gate_total = reduce_rows(dot(scaled_low, grad_gate, TN))
@@ -751,8 +820,12 @@
     grad_scan = jnp.concatenate([grad_joined.astype(bf16), ddt], axis=2).reshape(rows, -1)
     if fast:
         cut = grad_scan.shape[1] // 64 * 32
-        pieces = [gate_total, reduce_y(grad_scan[:, :cut]), reduce_x(grad_scan[:, cut:])]
-        in_total = jnp.concatenate(pieces, axis=0).astype(f32).T
+        first = near(grad_scan[:, :cut], by_y)
+        rest = near(grad_scan[:, cut:], by_x)
+        first = fold(fold(first, "fsdp", 1, 1), "seq", 2, 1)
+        rest = fold(fold(rest, "seq", 2, 1), "fsdp", 1, 1)
+        pairs = [gate_pair, spread_total(scatter_z(first, z)), spread_total(scatter_z(rest, z))]
+        in_total = place(slots, pairs, in_weight.shape[::-1]).T
     else:
         in_total = jnp.concatenate(
             [gate_total, reduce_rows(dot(scaled_low, grad_scan, TN))], axis=1

time: 519 us -> 509 us (0.981)
  waiting for transfers between devices: 155 us -> 206 us
  Pallas kernels: 103 us -> 75.2 us
  local copies, waits for them, and re-layouts: 51.2 us -> 27.6 us
  other arithmetic: 71 us -> 48.8 us
  starting transfers between devices: 88.8 us -> 95.6 us
    transpose x1 -> x0, other arithmetic: 23.1 us -> none  [per_device(): in_total = jnp.concatenate(pieces, axis=0).astype(f32).T]
    ppermute x31, waiting for transfers between devices: 123 us -> 145 us  [swap(): return lax.ppermute(x, axis, [(slot, slot ^ flip) for slot in range(count)])]
    ppermute x24, waiting for transfers between devices: 20.7 us -> 35.8 us  [ring(): lax.ppermute(x, 'seq', [(slot, (slot + 4 * shift) % 16) for slot in range...]
    all_to_all x1, waiting for transfers between devices: 0.01 us -> 13.8 us  [per_device(): lax.all_to_all(back_send, 'seq', split_axis=0, concat_axis=0, tiled=True)]
    pallas_call x1, Pallas kernels: 27.4 us -> 14 us  [scan_within_back(): call(within_back_body, seqs, [per_seq((length, channels)), per_seq((lengt...]
    pallas_call x0 -> x2, Pallas kernels: none -> 10.9 us  [place(): pl.pallas_call(functools.partial(place_body, bases), in_specs=[pl.BlockSp...]
    ppermute x6 -> x0, local copies, waits for them, and re-layouts: 9.98 us -> none  [ring(): lax.ppermute(x, 'seq', [(slot, (slot + 4 * shift) % 16) for slot in range...]
    pallas_call x1, Pallas kernels: 24 us -> 14.2 us  [scan_back(): call(back_body, seqs, [row, side, side, per_seq((length, channels)), per_...]
  transfers between devices with their start and end apart: 61 -> 61, of which waited for: 21 -> 31; matrix products, arithmetic and copies ran while one was open for 23% -> 18% of each run, Pallas kernels for 16% -> 4%
where the time goes in v2:
time: 509 us; the launch traced here: 500 us
  waiting for transfers between devices  206 us (40%)
  starting transfers between devices  95.6 us (19%)
  Pallas kernels  75.2 us (15%)
  other arithmetic  48.8 us (10%)
  matrix products  44.4 us (9%)
  local copies, waits for them, and re-layouts  27.6 us (5%)
    ppermute x31, waiting for transfers between devices, swap(): return lax.ppermute(x, axis, [(slot, slot ^ flip) for slot in range(count)])  145 us
    dot_general x16, matrix products, dot(): return lax.dot_general(a, b, (dims, ((), ())), preferred_element_type=f32)  44.4 us
    ppermute x24, waiting for transfers between devices, ring(): lax.ppermute(x, 'seq', [(slot, (slot + 4 * shift) % 16) for slot in range...  35.8 us
    ppermute x24, starting transfers between devices, ring(): lax.ppermute(x, 'seq', [(slot, (slot + 4 * shift) % 16) for slot in range...  35 us
    ppermute x31, starting transfers between devices, swap(): return lax.ppermute(x, axis, [(slot, slot ^ flip) for slot in range(count)])  31.3 us
    pallas_call x1, Pallas kernels, scan_back(): call(back_body, seqs, [row, side, side, per_seq((length, channels)), per_...  14.2 us
    pallas_call x1, Pallas kernels, scan_within_back(): call(within_back_body, seqs, [per_seq((length, channels)), per_seq((lengt...  14 us
    all_to_all x1, waiting for transfers between devices, per_device(): lax.all_to_all(back_send, 'seq', split_axis=0, concat_axis=0, tiled=True)  13.8 us
  transfers between devices with their start and end apart: 61, of which 31 were waited for; matrix products, arithmetic and copies ran while one was open for 18% of the time, Pallas kernels for 4%

profile of v2, /device:TPU:0, one launch (start us, length us, event | category | flops | bytes accessed | tf_op | source)
XLA Modules:
  0.0 499.8 jit_solution(2230059386909682455)
XLA Ops:
  0.7 2.8 slice_select_fusion
  3.5 3.0 collective-permute-start.1
  11.2 21.9 %collective-permute-done.1 = bf16[256,2336]{0,1:T(8,128)(2,1)} collective-permute-done((bf16[256,2336]{0,1:T(8,128)(2,1)}, bf16[256,2336]{0,1:T(8,128)(2,1)}, u32[]{:S(2)}, u32[]{:S(2)}) %collective-permute-start.1) | collective-permute-done | bytes 1196064 | tf_op jit(solution)/shard_map/ppermute | solution.py:589
  33.2 3.0 fusion.12
  36.2 2.0 convolution_add_fusion.1
  38.3 2.1 fusion.4
  40.4 8.7 %shard_map.194 = (f32[2,192,2304]{2,1,0:T(8,128)}, f32[2,192,32]{2,1,0:T(8,128)}, f32[2,192,32]{2,1,0:T(8,128)}, bf16[16,2,144,128]{3,2,1,0:T(8,128)(2,1)}) custom-call(bf16[2,208,2336]{2,1,0:T(8,128)(2,1)} %bitcast.49, f32[4,2304]{1,0:T(4,128)} %cw_ref.3, f32[1,2304]{1,0:T(1,128)} %broadcast_in_dim.10.cb_ref, f32[1,32]{1,0:T(1,128)} %bitcast.73, ...), custom_call_target="tpu_custom_call" | custom-call | flops 1207959552 | bytes 5308416 | tf_op jit(solution)/shard_map/pallas_call | solution.py:162
  53.9 6.0 %all-to-all-start = ((bf16[16,2,144,128]{3,2,1,0:T(8,128)(2,1)}), bf16[16,2,144,128]{3,2,1,0:T(8,128)(2,1)}, u32[]{:S(2)}, u32[]{:S(2)}) async-start(bf16[16,2,144,128]{3,2,1,0:T(8,128)(2,1)} %get-tuple-element.50), calls=%async_computation | async-start | bytes 2359296 | tf_op jit(solution)/shard_map/all_to_all | solution.py:757
  59.9 8.8 %shard_map.195.y_ref = f32[2,192,2048]{2,1,0:T(8,128)} custom-call(f32[2,192,2304]{2,1,0:T(8,128)} %get-tuple-element.47.conv_ref, f32[2,192,32]{2,1,0:T(8,128)} %get-tuple-element.48.dt_ref, f32[2,192,32]{2,1,0:T(8,128)} %get-tuple-element.49.cum_ref), custom_call_target="tpu_custom_call" | custom-call | flops 3623878656 | bytes 7077888 | tf_op jit(solution)/shard_map/pallas_call | solution.py:278
  68.7 7.7 %collective-permute-done.3 = bf16[256,2048]{0,1:T(8,128)(2,1)} collective-permute-done((bf16[256,2048]{0,1:T(8,128)(2,1)}, bf16[256,2048]{0,1:T(8,128)(2,1)}, u32[]{:S(2)}, u32[]{:S(2)}) %collective-permute-start.3) | collective-permute-done | bytes 1048608 | tf_op jit(solution)/shard_map/ppermute | solution.py:589
  79.2 19.4 %collective-permute-done.5 = bf16[512,1024]{1,0:T(8,128)(2,1)} collective-permute-done((bf16[512,1024]{1,0:T(8,128)(2,1)}, bf16[512,1024]{1,0:T(8,128)(2,1)}, u32[]{:S(2)}, u32[]{:S(2)}) %collective-permute-start.5) | collective-permute-done | bytes 1048608 | tf_op jit(solution)/shard_map/ppermute | solution.py:589
  101.2 3.0 broadcast_select_fusion.11
  104.3 2.6 shard_map.196
  106.8 6.4 %all-to-all-start.1 = ((bf16[16,2,128,128]{3,2,1,0:T(8,128)(2,1)}), bf16[16,2,128,128]{3,2,1,0:T(8,128)(2,1)S(1)}, u32[]{:S(2)}, u32[]{:S(2)}) async-start(bf16[16,2,128,128]{3,2,1,0:T(8,128)(2,1)} %get-tuple-element.51), calls=%async_computation.1 | async-start | bytes 2097152 | tf_op jit(solution)/shard_map/all_to_all | solution.py:763
  118.8 3.0 convolution_convert_fusion.4
  121.7 3.5 fusion.10
  125.3 10.9 %all-to-all-done.1.start_ref = bf16[16,2,128,128]{3,2,1,0:T(8,128)(2,1)S(1)} async-done(((bf16[16,2,128,128]{3,2,1,0:T(8,128)(2,1)}), bf16[16,2,128,128]{3,2,1,0:T(8,128)(2,1)S(1)}, u32[]{:S(2)}, u32[]{:S(2)}) %all-to-all-start.1) | async-done | bytes 1048608 | tf_op jit(solution)/shard_map/all_to_all | solution.py:763
  137.2 13.6 %shard_map.197 = (bf16[2,192,2048]{2,1,0:T(8,128)(2,1)}, bf16[2,192,2048]{2,1,0:T(8,128)(2,1)}, bf16[2,192,2048]{2,1,0:T(8,128)(2,1)}, bf16[16,2,128,128]{3,2,1,...) custom-call(f32[2,192,2048]{2,1,0:T(8,128)} %shard_map.195.y_ref, ...), custom_call_target="tpu_custom_call" | custom-call | flops 1207959552 | bytes 17694720 | tf_op jit(solution)/shard_map/pallas_call | solution.py:359
  150.7 14.0 %shard_map.198 = (f32[2,192,2048]{2,1,0:T(8,128)}, f32[2,192,128]{2,1,0:T(8,128)}, f32[2,192,128]{2,1,0:T(8,128)}) custom-call(f32[2,192,2304]{2,1,0:T(8,128)} %get-tuple-element.47.conv_ref, f32[2,192,32]{2,1,0:T(8,128)} %get-tuple-element.48.dt_ref, f32[2,192,32]{2,1,0:T(8,128)} %get-tuple-element.49.cum_ref, ...), custom_call_target="tpu_custom_call" | custom-call | flops 7247757312 | bytes 8847360 | tf_op jit(solution)/shard_map/pallas_call | solution.py:443
  165.8 2.6 convolution_convert_fusion.3
  170.4 6.5 %all-to-all-start.2 = ((bf16[16,2,128,128]{3,2,1,0:T(8,128)(2,1)}), bf16[16,2,128,128]{3,2,1,0:T(8,128)(2,1)S(1)}, u32[]{:S(2)}, u32[]{:S(2)}) async-start(bf16[16,2,128,128]{3,2,1,0:T(8,128)(2,1)} %get-tuple-element.66), calls=%async_computation.2 | async-start | bytes 2097152 | tf_op jit(solution)/shard_map/all_to_all | solution.py:770
  177.0 3.7 convolution_convert_fusion.2
  186.1 13.8 %all-to-all-done.2.recv_ref = bf16[16,2,128,128]{3,2,1,0:T(8,128)(2,1)S(1)} async-done(((bf16[16,2,128,128]{3,2,1,0:T(8,128)(2,1)}), bf16[16,2,128,128]{3,2,1,0:T(8,128)(2,1)S(1)}, u32[]{:S(2)}, u32[]{:S(2)}) %all-to-all-start.2) | async-done | bytes 1048608 | tf_op jit(solution)/shard_map/all_to_all | solution.py:770
  200.9 2.5 shard_map.199
  203.3 7.0 %all-to-all-start.3 = ((bf16[16,2,128,128]{3,2,1,0:T(8,128)(2,1)}), bf16[16,2,128,128]{3,2,1,0:T(8,128)(2,1)S(1)}, u32[]{:S(2)}, u32[]{:S(2)}) async-start(bf16[16,2,128,128]{3,2,1,0:T(8,128)(2,1)} %shard_map.199), calls=%async_computation.3 | async-start | bytes 2097152 | tf_op jit(solution)/shard_map/all_to_all | solution.py:773
  210.4 3.6 convert_add_fusion.1
  216.8 2.9 convert_add_fusion
  224.3 3.2 broadcast_select_fusion.1
  228.9 5.8 %fusion.11 = f32[384,1024]{1,0:T(8,128)} fusion(bf16[384,2048]{1,0:T(8,128)(2,1)} %bitcast.63, bf16[512,2048]{0,1:T(8,128)(2,1)} %copy-done.32, bf16[512,2048]{0,1:T(8,128)(2,1)} %copy-done.31), kind=kOutput, calls=%fused_computation.25 | convolution fusion | flops 1619001344 | bytes 7340032 | tf_op jit(solution)/shard_map/dot_general | solution.py:708
  234.7 6.8 %collective-permute-done.8 = bf16[1024,512]{1,0:T(8,128)(2,1)} collective-permute-done((bf16[1024,512]{1,0:T(8,128)(2,1)}, bf16[1024,512]{1,0:T(8,128)(2,1)}, u32[]{:S(2)}, u32[]{:S(2)}) %collective-permute-start.8) | collective-permute-done | bytes 1048608 | tf_op jit(solution)/shard_map/ppermute | solution.py:589
  241.5 2.9 slice_add_fusion.1
  244.4 19.2 %collective-permute-done.10 = bf16[2048,256]{1,0:T(8,128)(2,1)} collective-permute-done((bf16[2048,256]{1,0:T(8,128)(2,1)}, bf16[2048,256]{1,0:T(8,128)(2,1)}, u32[]{:S(2)}, u32[]{:S(2)}) %collective-permute-start.10) | collective-permute-done | bytes 1048608 | tf_op jit(solution)/shard_map/ppermute | solution.py:589
  263.6 3.0 slice_add_fusion
  267.5 14.2 %shard_map.200 = (f32[2,192,2304]{2,1,0:T(8,128)}, bf16[2,192,32]{2,1,0:T(8,128)(2,1)}, f32[2,4,2304]{2,1,0:T(4,128)}, f32[2,1,2304]{2,1,0:T(1,128)}, f32[2,1,32]{2,1,0:T(1,128)}, /*index=5*/f32[2,1,32]{2,1,0:T(1,128)}) custom-call(f32[2,192,2048]{2,1,0:T(8,128)} %get-tuple-element.60.u_ref, f32[2,192,128]{2,1,0:T(8,128)} %get-tuple-element.61.dw_ref, ...), custom_call_target="tpu_custom_call" | custom-call | flops 1006632960 | bytes 21233664 | tf_op jit(solution)/shard_map/pallas_call | solution.py:546
  285.1 4.0 constant_dynamic-update-slice_fusion.1
  297.3 6.0 %fusion.7 = bf16[2,192,2304]{2,1,0:T(8,128)(2,1)S(1)} fusion(f32[2,200,2304]{2,1,0:T(8,128)} %constant_dynamic-update-slice_fusion, f32[2,192,2304]{2,1,0:T(8,128)S(1)} %copy-done.2, f32[2304]{0:T(1024)} %get-tuple-element.83, f32[2304]{0:T(1024)} %get-tuple-element.84, f32[2304]{0:T(1024)} %get-tuple-element.82, f32[2304]{0:T(1024)S(1)} %get-tuple-element.81), kind=kLoop, calls=%fused_computation.14 | loop fusion | flops 7077888 | bytes 15962112 | tf_op jit(solution)/shard_map/convert_element_type | solution.py:820
  305.2 3.5 fusion.21
  310.1 5.4 %fusion.17 = bf16[384,1024]{1,0:T(8,128)(2,1)} fusion(bf16[2,192,1024]{2,1,0:T(8,128)(2,1)S(1)} %copy-done.7, bf16[384,2048]{1,0:T(8,128)(2,1)} %bitcast.66, bf16[1024,1024]{1,0:T(8,128)(2,1)} %copy-done.30, bf16[1024,1024]{1,0:T(8,128)(2,1)} %copy-done.29), kind=kOutput, calls=%fused_computation.54 | convolution fusion | flops 1620180992 | bytes 7340032 | tf_op jit(solution)/shard_map/dot_general | solution.py:708
  320.6 21.5 %collective-permute-done.13 = f32[14688]{0:T(1024)S(1)} collective-permute-done((f32[14688]{0:T(1024)S(1)}, f32[14688]{0:T(1024)S(1)}, u32[]{:S(2)}, u32[]{:S(2)}) %collective-permute-start.13) | collective-permute-done | bytes 58784 | tf_op jit(solution)/shard_map/ppermute | solution.py:589
  342.1 2.2 collective-permute-start.14
  346.7 3.9 collective-permute-start.20
  352.0 2.5 collective-permute-done.20
  354.6 4.3 collective-permute-start.51
  358.9 4.0 collective-permute-done.19
  362.9 4.8 collective-permute-start.49
  367.9 5.9 %collective-permute-done.50 = bf16[256,256]{1,0:T(8,128)(2,1)S(1)} collective-permute-done((bf16[256,256]{1,0:T(8,128)(2,1)S(1)}, bf16[256,256]{1,0:T(8,128)(2,1)S(1)}, u32[]{:S(2)}, u32[]{:S(2)}) %collective-permute-start.50) | collective-permute-done | bytes 131104 | tf_op jit(solution)/shard_map/ppermute | solution.py:653
  373.8 5.2 %collective-permute-start.21 = (bf16[512,128]{1,0:T(8,128)(2,1)S(1)}, bf16[512,128]{1,0:T(8,128)(2,1)S(1)}, u32[]{:S(2)}, u32[]{:S(2)}) collective-permute-start(bf16[512,128]{1,0:T(8,128)(2,1)S(1)} %add_convert_fusion.1), channel_id=1, source_target_pairs={{0,8},{2,10},{4,12},{6,14},{8,16},{10,18},{12,20},{14,22},{16,24},... | collective-permute-start | bytes 393224 | tf_op jit(solution)/shard_map/ppermute | solution.py:653
  379.2 6.1 %collective-permute-done.22 = bf16[512,128]{1,0:T(8,128)(2,1)S(1)} collective-permute-done((bf16[512,128]{1,0:T(8,128)(2,1)S(1)}, bf16[512,128]{1,0:T(8,128)(2,1)S(1)}, u32[]{:S(2)}, u32[]{:S(2)}) %collective-permute-start.22) | collective-permute-done | bytes 131104 | tf_op jit(solution)/shard_map/ppermute | solution.py:653
  385.3 5.0 collective-permute-start.52
  390.4 3.4 collective-permute-start.15
  393.8 3.1 collective-permute-done.53
  403.3 8.5 %collective-permute-done.24 = bf16[2048,128]{1,0:T(8,128)(2,1)S(1)} collective-permute-done((bf16[2048,128]{1,0:T(8,128)(2,1)S(1)}, bf16[2048,128]{1,0:T(8,128)(2,1)S(1)}, u32[]{:S(2)}, u32[]{:S(2)}) %collective-permute-start.24) | collective-permute-done | bytes 524320 | tf_op jit(solution)/shard_map/ppermute | solution.py:589
  413.9 22.1 %collective-permute-done.38 = bf16[1184,256]{1,0:T(8,128)(2,1)S(1)} collective-permute-done((bf16[1184,256]{1,0:T(8,128)(2,1)S(1)}, bf16[1184,256]{1,0:T(8,128)(2,1)S(1)}, u32[]{:S(2)}, u32[]{:S(2)}) %collective-permute-start.38) | collective-permute-done | bytes 606240 | tf_op jit(solution)/shard_map/ppermute | solution.py:589
  440.1 3.0 collective-permute-done.39
  443.3 3.2 collective-permute-done.31
  447.7 2.2 collective-permute-done.29
  449.9 2.1 collective-permute-done.42
  452.0 2.5 collective-permute-start.34
  458.9 2.5 collective-permute-start.45
  464.8 2.8 collective-permute-done.44
  470.1 7.4 %collective-permute-done.35 = bf16[1152,128]{1,0:T(8,128)(2,1)S(1)} collective-permute-done((bf16[1152,128]{1,0:T(8,128)(2,1)S(1)}, bf16[1152,128]{1,0:T(8,128)(2,1)S(1)}, u32[]{:S(2)}, u32[]{:S(2)}) %collective-permute-start.35) | collective-permute-done | bytes 294944 | tf_op jit(solution)/shard_map/ppermute | solution.py:589
  478.4 2.3 collective-permute-done.46
  488.5 3.9 shard_map.202
  492.3 7.0 %shard_map.201 = f32[4384,512]{1,0:T(8,128)} custom-call(s32[3]{0:T(128)} %pad_add_fusion.slots_ref, bf16[2048,256]{1,0:T(8,128)(2,1)} %copy-done.19, bf16[2048,256]{1,0:T(8,128)(2,1)} %collective-permute-done.25.refs_1_, bf16[1152,256]{1,0:T(8,128)(2,1)} %pad_maximum_fusion.21.refs_2_, bf16[1152,256]{1,0:T(8,128)(2,1)} %collective-permute-done.36.refs_3_, ...), custom_call_target="tpu_custom_call" | custom-call | bytes 13467648 | tf_op jit(solution)/shard_map/pallas_call | solution.py:694
  (317 shorter events, 96.8 us)
Async XLA Ops:
  3.5 29.6 %collective-permute-start.1 = (bf16[256,2336]{0,1:T(8,128)(2,1)}, bf16[256,2336]{0,1:T(8,128)(2,1)}, u32[]{:S(2)}, u32[]{:S(2)}) collective-permute-start(bf16[256,2336]{0,1:T(8,128)(2,1)} %slice_select_fusion), channel_id=1, source_target_pairs={{0,1},{1,0},{2,3},{3,2},{4,5},{5,4},{6,7},{7,6},{8,9},{9,8},{10,11... | collective-permute-start | bytes 3588104 | tf_op jit(solution)/shard_map/ppermute | solution.py:589
  7.0 69.5 %copy-start.8 = (bf16[2,192,1024]{2,1,0:T(8,128)(2,1)}, bf16[2,192,1024]{2,1,0:T(8,128)(2,1)S(1)}, u32[]{:S(2)}) copy-start(bf16[2,192,1024]{2,1,0:T(8,128)(2,1)S(1)} %fusion.16) | copy-start | bytes 2359300
  7.0 4.0 collective-permute-start
  33.1 5.1 %collective-permute-start.2 = (bf16[256,2336]{0,1:T(8,128)(2,1)}, bf16[256,2336]{0,1:T(8,128)(2,1)S(1)}, u32[]{:S(2)}, u32[]{:S(2)}) collective-permute-start(bf16[256,2336]{0,1:T(8,128)(2,1)} %collective-permute-done.1), channel_id=1, source_target_pairs={{0,2},{2,0},{4,6},{6,4},{8,10},{10,8},{12,14},{14,12},{16,18},{18,... | collective-permute-start | bytes 3588104 | tf_op jit(solution)/shard_map/ppermute | solution.py:589
  50.2 26.3 %collective-permute-start.3 = (bf16[256,2048]{0,1:T(8,128)(2,1)}, bf16[256,2048]{0,1:T(8,128)(2,1)}, u32[]{:S(2)}, u32[]{:S(2)}) collective-permute-start(bf16[256,2048]{0,1:T(8,128)(2,1)} %slice_select_fusion.2), channel_id=1, source_target_pairs={{0,1},{1,0},{2,3},{3,2},{4,5},{5,4},{6,7},{7,6},{8,9},{9,8},{10,11... | collective-permute-start | bytes 3145736 | tf_op jit(solution)/shard_map/ppermute | solution.py:589
  53.0 45.5 %collective-permute-start.5 = (bf16[512,1024]{1,0:T(8,128)(2,1)}, bf16[512,1024]{1,0:T(8,128)(2,1)}, u32[]{:S(2)}, u32[]{:S(2)}) collective-permute-start(bf16[512,1024]{1,0:T(8,128)(2,1)} %slice_select_fusion.1), channel_id=1, source_target_pairs={{0,1},{1,0},{2,3},{3,2},{4,5},{5,4},{6,7},{7,6},{8,9},{9,8},{10,11... | collective-permute-start | bytes 3145736 | tf_op jit(solution)/shard_map/ppermute | solution.py:589
  53.9 50.3 %all-to-all-start = ((bf16[16,2,144,128]{3,2,1,0:T(8,128)(2,1)}), bf16[16,2,144,128]{3,2,1,0:T(8,128)(2,1)}, u32[]{:S(2)}, u32[]{:S(2)}) async-start(bf16[16,2,144,128]{3,2,1,0:T(8,128)(2,1)} %get-tuple-element.50), calls=%async_computation | async-start | bytes 2359296 | tf_op jit(solution)/shard_map/all_to_all | solution.py:757
  76.5 24.8 %collective-permute-start.4 = (bf16[256,2048]{0,1:T(8,128)(2,1)}, bf16[256,2048]{0,1:T(8,128)(2,1)}, u32[]{:S(2)}, u32[]{:S(2)}) collective-permute-start(bf16[256,2048]{0,1:T(8,128)(2,1)} %collective-permute-done.3), channel_id=1, source_target_pairs={{0,2},{2,0},{4,6},{6,4},{8,10},{10,8},{12,14},{14,12},{16,18},{18,... | collective-permute-start | bytes 3145736 | tf_op jit(solution)/shard_map/ppermute | solution.py:589
  98.6 14.7 %collective-permute-start.6 = (bf16[512,1024]{1,0:T(8,128)(2,1)}, bf16[512,1024]{1,0:T(8,128)(2,1)}, u32[]{:S(2)}, u32[]{:S(2)}) collective-permute-start(bf16[512,1024]{1,0:T(8,128)(2,1)} %collective-permute-done.5), channel_id=1, source_target_pairs={{0,2},{2,0},{4,6},{6,4},{8,10},{10,8},{12,14},{14,12},{16,18},{18,... | collective-permute-start | bytes 3145736 | tf_op jit(solution)/shard_map/ppermute | solution.py:589
  106.8 29.4 %all-to-all-start.1 = ((bf16[16,2,128,128]{3,2,1,0:T(8,128)(2,1)}), bf16[16,2,128,128]{3,2,1,0:T(8,128)(2,1)S(1)}, u32[]{:S(2)}, u32[]{:S(2)}) async-start(bf16[16,2,128,128]{3,2,1,0:T(8,128)(2,1)} %get-tuple-element.51), calls=%async_computation.1 | async-start | bytes 2097152 | tf_op jit(solution)/shard_map/all_to_all | solution.py:763
  168.5 41.9 %collective-permute-start.7 = (bf16[2048,512]{1,0:T(8,128)(2,1)}, bf16[2048,512]{1,0:T(8,128)(2,1)}, u32[]{:S(2)}, u32[]{:S(2)}) collective-permute-start(bf16[2048,512]{1,0:T(8,128)(2,1)} %convolution_convert_fusion.3), channel_id=1, source_target_pairs={{0,2},{2,0},{4,6},{6,4},{8,10},{10,8},{12,14},{14,12},{16,18},{18,... | collective-permute-start | bytes 6291464 | tf_op jit(solution)/shard_map/ppermute | solution.py:589
  170.4 29.5 %all-to-all-start.2 = ((bf16[16,2,128,128]{3,2,1,0:T(8,128)(2,1)}), bf16[16,2,128,128]{3,2,1,0:T(8,128)(2,1)S(1)}, u32[]{:S(2)}, u32[]{:S(2)}) async-start(bf16[16,2,128,128]{3,2,1,0:T(8,128)(2,1)} %get-tuple-element.66), calls=%async_computation.2 | async-start | bytes 2097152 | tf_op jit(solution)/shard_map/all_to_all | solution.py:770
  180.7 36.1 %collective-permute-start.9 = (bf16[2048,512]{1,0:T(8,128)(2,1)}, bf16[2048,512]{1,0:T(8,128)(2,1)}, u32[]{:S(2)}, u32[]{:S(2)}) collective-permute-start(bf16[2048,512]{1,0:T(8,128)(2,1)} %convolution_convert_fusion.2), channel_id=1, source_target_pairs={{0,2},{2,0},{4,6},{6,4},{8,10},{10,8},{12,14},{14,12},{16,18},{18,... | collective-permute-start | bytes 6291464 | tf_op jit(solution)/shard_map/ppermute | solution.py:589
  203.3 63.2 %all-to-all-start.3 = ((bf16[16,2,128,128]{3,2,1,0:T(8,128)(2,1)}), bf16[16,2,128,128]{3,2,1,0:T(8,128)(2,1)S(1)}, u32[]{:S(2)}, u32[]{:S(2)}) async-start(bf16[16,2,128,128]{3,2,1,0:T(8,128)(2,1)} %shard_map.199), calls=%async_computation.3 | async-start | bytes 2097152 | tf_op jit(solution)/shard_map/all_to_all | solution.py:773
  215.2 26.3 %collective-permute-start.8 = (bf16[1024,512]{1,0:T(8,128)(2,1)}, bf16[1024,512]{1,0:T(8,128)(2,1)}, u32[]{:S(2)}, u32[]{:S(2)}) collective-permute-start(bf16[1024,512]{1,0:T(8,128)(2,1)} %slice.460), channel_id=1, source_target_pairs={{0,1},{1,0},{2,3},{3,2},{4,5},{5,4},{6,7},{7,6},{8,9},{9,8},{10,11... | collective-permute-start | bytes 3145736 | tf_op jit(solution)/shard_map/ppermute | solution.py:589
  222.9 40.7 %collective-permute-start.10 = (bf16[2048,256]{1,0:T(8,128)(2,1)}, bf16[2048,256]{1,0:T(8,128)(2,1)}, u32[]{:S(2)}, u32[]{:S(2)}) collective-permute-start(bf16[2048,256]{1,0:T(8,128)(2,1)} %slice.459), channel_id=1, source_target_pairs={{0,1},{1,0},{2,3},{3,2},{4,5},{5,4},{6,7},{7,6},{8,9},{9,8},{10,11... | collective-permute-start | bytes 3145736 | tf_op jit(solution)/shard_map/ppermute | solution.py:589
  283.3 12.3 %collective-permute-start.11 = (f32[2,8,2304]{2,1,0:T(8,128)}, f32[2,8,2304]{2,1,0:T(8,128)}, u32[]{:S(2)}, u32[]{:S(2)}) collective-permute-start(f32[2,8,2304]{2,1,0:T(8,128)} %slice.254), channel_id=1, source_target_pairs={{2,0},{4,2},{6,4},{8,6},{10,8},{12,10},{14,12},{16,14},{18,16},{20... | collective-permute-start | bytes 442376 | tf_op jit(solution)/shard_map/ppermute | solution.py:814
  308.9 9.0 %collective-permute-start.12 = (f32[14688]{0:T(1024)S(1)}, f32[14688]{0:T(1024)S(1)}, u32[]{:S(2)}, u32[]{:S(2)}) collective-permute-start(f32[14688]{0:T(1024)S(1)} %concatenate.89), channel_id=1, source_target_pairs={{0,2},{2,0},{4,6},{6,4},{8,10},{10,8},{12,14},{14,12},{16,18},{18,... | collective-permute-start | bytes 176264 | tf_op jit(solution)/shard_map/ppermute | solution.py:589
  315.6 30.9 %collective-permute-start.17 = (bf16[2048,128]{1,0:T(8,128)(2,1)S(1)}, bf16[2048,128]{1,0:T(8,128)(2,1)S(1)}, u32[]{:S(2)}, u32[]{:S(2)}) collective-permute-start(bf16[2048,128]{1,0:T(8,128)(2,1)S(1)} %slice.464), channel_id=1, source_target_pairs={{0,4},{2,6},{4,0},{6,2},{8,12},{10,14},{12,8},{14,10},{16,20},{18,... | collective-permute-start | bytes 1572872 | tf_op jit(solution)/shard_map/ppermute | solution.py:589
  317.6 33.0 %collective-permute-start.48 = (bf16[1024,256]{1,0:T(8,128)(2,1)S(1)}, bf16[1024,256]{1,0:T(8,128)(2,1)S(1)}, u32[]{:S(2)}, u32[]{:S(2)}) collective-permute-start(bf16[1024,256]{1,0:T(8,128)(2,1)S(1)} %slice.463), channel_id=1, source_target_pairs={{0,4},{2,6},{4,0},{6,2},{8,12},{10,14},{12,8},{14,10},{16,20},{18,... | collective-permute-start | bytes 1572872 | tf_op jit(solution)/shard_map/ppermute | solution.py:589
  317.8 24.3 %collective-permute-start.13 = (f32[14688]{0:T(1024)S(1)}, f32[14688]{0:T(1024)S(1)}, u32[]{:S(2)}, u32[]{:S(2)}) collective-permute-start(f32[14688]{0:T(1024)S(1)} %add.260), channel_id=1, source_target_pairs={{0,4},{2,6},{4,0},{6,2},{8,12},{10,14},{12,8},{14,10},{16,20},{18,... | collective-permute-start | bytes 176264 | tf_op jit(solution)/shard_map/ppermute | solution.py:589
  342.1 4.4 collective-permute-start.14
  345.1 54.0 %collective-permute-start.26 = (bf16[1152,512]{1,0:T(8,128)(2,1)S(1)}, bf16[1152,512]{1,0:T(8,128)(2,1)S(1)}, u32[]{:S(2)}, u32[]{:S(2)}) collective-permute-start(bf16[1152,512]{1,0:T(8,128)(2,1)S(1)} %convolution_convert_fusion.1), channel_id=1, source_target_pairs={{0,2},{2,0},{4,6},{6,4},{8,10},{10,8},{12,14},{14,12},{16,18},{18,... | collective-permute-start | bytes 3538952 | tf_op jit(solution)/shard_map/ppermute | solution.py:589
  345.2 56.4 %collective-permute-start.37 = (bf16[1184,512]{1,0:T(8,128)(2,1)S(1)}, bf16[1184,512]{1,0:T(8,128)(2,1)S(1)}, u32[]{:S(2)}, u32[]{:S(2)}) collective-permute-start(bf16[1184,512]{1,0:T(8,128)(2,1)S(1)} %convolution_convert_fusion), channel_id=1, source_target_pairs={{0,2},{2,0},{4,6},{6,4},{8,10},{10,8},{12,14},{14,12},{16,18},{18,... | collective-permute-start | bytes 3637256 | tf_op jit(solution)/shard_map/ppermute | solution.py:589
  346.7 7.8 %collective-permute-start.20 = (bf16[512,128]{1,0:T(8,128)(2,1)S(1)}, bf16[512,128]{1,0:T(8,128)(2,1)S(1)}, u32[]{:S(2)}, u32[]{:S(2)}) collective-permute-start(bf16[512,128]{1,0:T(8,128)(2,1)S(1)} %get-tuple-element.103), channel_id=1, source_target_pairs={{0,24},{2,26},{4,28},{6,30},{8,0},{10,2},{12,4},{14,6},{16,8},{18,... | collective-permute-start | bytes 393224 | tf_op jit(solution)/shard_map/ppermute | solution.py:653
  350.6 12.3 %collective-permute-start.19 = (bf16[512,128]{1,0:T(8,128)(2,1)S(1)}, bf16[512,128]{1,0:T(8,128)(2,1)S(1)}, u32[]{:S(2)}, u32[]{:S(2)}) collective-permute-start(bf16[512,128]{1,0:T(8,128)(2,1)S(1)} %get-tuple-element.104), channel_id=1, source_target_pairs={{0,16},{2,18},{4,20},{6,22},{8,24},{10,26},{12,28},{14,30},{16,0},... | collective-permute-start | bytes 393224 | tf_op jit(solution)/shard_map/ppermute | solution.py:653
  350.6 12.3 %collective-permute-start.18 = (bf16[512,128]{1,0:T(8,128)(2,1)S(1)}, bf16[512,128]{1,0:T(8,128)(2,1)S(1)}, u32[]{:S(2)}, u32[]{:S(2)}) collective-permute-start(bf16[512,128]{1,0:T(8,128)(2,1)S(1)} %get-tuple-element.102), channel_id=1, source_target_pairs={{0,8},{2,10},{4,12},{6,14},{8,16},{10,18},{12,20},{14,22},{16,24},... | collective-permute-start | bytes 393224 | tf_op jit(solution)/shard_map/ppermute | solution.py:653
  351.9 47.2 %copy-start.36 = (bf16[384,128]{1,0:T(8,128)(2,1)S(1)}, bf16[384,128]{1,0:T(8,128)(2,1)}, u32[]{:S(2)}) copy-start(bf16[384,128]{1,0:T(8,128)(2,1)} %get-tuple-element.125) | copy-start | bytes 294916
  354.6 13.3 %collective-permute-start.51 = (bf16[256,256]{1,0:T(8,128)(2,1)S(1)}, bf16[256,256]{1,0:T(8,128)(2,1)S(1)}, u32[]{:S(2)}, u32[]{:S(2)}) collective-permute-start(bf16[256,256]{1,0:T(8,128)(2,1)S(1)} %get-tuple-element.100), channel_id=1, source_target_pairs={{0,24},{2,26},{4,28},{6,30},{8,0},{10,2},{12,4},{14,6},{16,8},{18,... | collective-permute-start | bytes 393224 | tf_op jit(solution)/shard_map/ppermute | solution.py:653
  362.9 10.9 %collective-permute-start.50 = (bf16[256,256]{1,0:T(8,128)(2,1)S(1)}, bf16[256,256]{1,0:T(8,128)(2,1)S(1)}, u32[]{:S(2)}, u32[]{:S(2)}) collective-permute-start(bf16[256,256]{1,0:T(8,128)(2,1)S(1)} %get-tuple-element.101), channel_id=1, source_target_pairs={{0,16},{2,18},{4,20},{6,22},{8,24},{10,26},{12,28},{14,30},{16,0},... | collective-permute-start | bytes 393224 | tf_op jit(solution)/shard_map/ppermute | solution.py:653
  362.9 10.9 %collective-permute-start.49 = (bf16[256,256]{1,0:T(8,128)(2,1)S(1)}, bf16[256,256]{1,0:T(8,128)(2,1)S(1)}, u32[]{:S(2)}, u32[]{:S(2)}) collective-permute-start(bf16[256,256]{1,0:T(8,128)(2,1)S(1)} %get-tuple-element.99), channel_id=1, source_target_pairs={{0,8},{2,10},{4,12},{6,14},{8,16},{10,18},{12,20},{14,22},{16,24},... | collective-permute-start | bytes 393224 | tf_op jit(solution)/shard_map/ppermute | solution.py:653
  367.8 11.3 %collective-permute-start.23 = (bf16[512,128]{1,0:T(8,128)(2,1)S(1)}, bf16[512,128]{1,0:T(8,128)(2,1)S(1)}, u32[]{:S(2)}, u32[]{:S(2)}) collective-permute-start(bf16[512,128]{1,0:T(8,128)(2,1)S(1)} %add_convert_fusion.1), channel_id=1, source_target_pairs={{0,24},{2,26},{4,28},{6,30},{8,0},{10,2},{12,4},{14,6},{16,8},{18,... | collective-permute-start | bytes 393224 | tf_op jit(solution)/shard_map/ppermute | solution.py:653
  373.8 11.5 %collective-permute-start.22 = (bf16[512,128]{1,0:T(8,128)(2,1)S(1)}, bf16[512,128]{1,0:T(8,128)(2,1)S(1)}, u32[]{:S(2)}, u32[]{:S(2)}) collective-permute-start(bf16[512,128]{1,0:T(8,128)(2,1)S(1)} %add_convert_fusion.1), channel_id=1, source_target_pairs={{0,16},{2,18},{4,20},{6,22},{8,24},{10,26},{12,28},{14,30},{16,0},... | collective-permute-start | bytes 393224 | tf_op jit(solution)/shard_map/ppermute | solution.py:653
  373.8 11.5 %collective-permute-start.21 = (bf16[512,128]{1,0:T(8,128)(2,1)S(1)}, bf16[512,128]{1,0:T(8,128)(2,1)S(1)}, u32[]{:S(2)}, u32[]{:S(2)}) collective-permute-start(bf16[512,128]{1,0:T(8,128)(2,1)S(1)} %add_convert_fusion.1), channel_id=1, source_target_pairs={{0,8},{2,10},{4,12},{6,14},{8,16},{10,18},{12,20},{14,22},{16,24},... | collective-permute-start | bytes 393224 | tf_op jit(solution)/shard_map/ppermute | solution.py:653
  379.1 11.2 %collective-permute-start.54 = (bf16[256,256]{1,0:T(8,128)(2,1)S(1)}, bf16[256,256]{1,0:T(8,128)(2,1)S(1)}, u32[]{:S(2)}, u32[]{:S(2)}) collective-permute-start(bf16[256,256]{1,0:T(8,128)(2,1)S(1)} %add_convert_fusion), channel_id=1, source_target_pairs={{0,24},{2,26},{4,28},{6,30},{8,0},{10,2},{12,4},{14,6},{16,8},{18,... | collective-permute-start | bytes 393224 | tf_op jit(solution)/shard_map/ppermute | solution.py:653
  385.3 11.6 %collective-permute-start.53 = (bf16[256,256]{1,0:T(8,128)(2,1)S(1)}, bf16[256,256]{1,0:T(8,128)(2,1)S(1)}, u32[]{:S(2)}, u32[]{:S(2)}) collective-permute-start(bf16[256,256]{1,0:T(8,128)(2,1)S(1)} %add_convert_fusion), channel_id=1, source_target_pairs={{0,16},{2,18},{4,20},{6,22},{8,24},{10,26},{12,28},{14,30},{16,0},... | collective-permute-start | bytes 393224 | tf_op jit(solution)/shard_map/ppermute | solution.py:653
  385.3 12.4 %collective-permute-start.52 = (bf16[256,256]{1,0:T(8,128)(2,1)S(1)}, bf16[256,256]{1,0:T(8,128)(2,1)S(1)}, u32[]{:S(2)}, u32[]{:S(2)}) collective-permute-start(bf16[256,256]{1,0:T(8,128)(2,1)S(1)} %add_convert_fusion), channel_id=1, source_target_pairs={{0,8},{2,10},{4,12},{6,14},{8,16},{10,18},{12,20},{14,22},{16,24},... | collective-permute-start | bytes 393224 | tf_op jit(solution)/shard_map/ppermute | solution.py:653
  390.4 90.5 %collective-permute-start.15 = (f32[14688]{0:T(1024)S(1)}, f32[14688]{0:T(1024)S(1)}, u32[]{:S(2)}, u32[]{:S(2)}) collective-permute-start(f32[14688]{0:T(1024)S(1)} %add.262), channel_id=1, source_target_pairs={{0,16},{2,18},{4,20},{6,22},{8,24},{10,26},{12,28},{14,30},{16,0},... | collective-permute-start | bytes 176264 | tf_op jit(solution)/shard_map/ppermute | solution.py:589
  397.0 14.9 %collective-permute-start.24 = (bf16[2048,128]{1,0:T(8,128)(2,1)S(1)}, bf16[2048,128]{1,0:T(8,128)(2,1)S(1)}, u32[]{:S(2)}, u32[]{:S(2)}) collective-permute-start(bf16[2048,128]{1,0:T(8,128)(2,1)S(1)} %pad_maximum_fusion.22), channel_id=1, source_target_pairs={{0,4},{2,6},{4,0},{6,2},{8,12},{10,14},{12,8},{14,10},{16,20},{18,... | collective-permute-start | bytes 1572872 | tf_op jit(solution)/shard_map/ppermute | solution.py:589
  397.7 72.2 %collective-permute-start.55 = (bf16[1024,256]{1,0:T(8,128)(2,1)S(1)}, bf16[1024,256]{1,0:T(8,128)(2,1)S(1)}, u32[]{:S(2)}, u32[]{:S(2)}) collective-permute-start(bf16[1024,256]{1,0:T(8,128)(2,1)S(1)} %pad_maximum_fusion.23), channel_id=1, source_target_pairs={{0,4},{2,6},{4,0},{6,2},{8,12},{10,14},{12,8},{14,10},{16,20},{18,... | collective-permute-start | bytes 1572872 | tf_op jit(solution)/shard_map/ppermute | solution.py:589
  400.0 13.3 %collective-permute-start.27 = (bf16[1152,256]{1,0:T(8,128)(2,1)S(1)}, bf16[1152,256]{1,0:T(8,128)(2,1)S(1)}, u32[]{:S(2)}, u32[]{:S(2)}) collective-permute-start(bf16[1152,256]{1,0:T(8,128)(2,1)S(1)} %slice.462), channel_id=1, source_target_pairs={{0,1},{1,0},{2,3},{3,2},{4,5},{5,4},{6,7},{7,6},{8,9},{9,8},{10,11... | collective-permute-start | bytes 1769480 | tf_op jit(solution)/shard_map/ppermute | solution.py:589
  402.5 33.5 %collective-permute-start.38 = (bf16[1184,256]{1,0:T(8,128)(2,1)S(1)}, bf16[1184,256]{1,0:T(8,128)(2,1)S(1)}, u32[]{:S(2)}, u32[]{:S(2)}) collective-permute-start(bf16[1184,256]{1,0:T(8,128)(2,1)S(1)} %slice.461), channel_id=1, source_target_pairs={{0,4},{2,6},{4,0},{6,2},{8,12},{10,14},{12,8},{14,10},{16,20},{18,... | collective-permute-start | bytes 1818632 | tf_op jit(solution)/shard_map/ppermute | solution.py:589
  411.9 52.8 %copy-start.19 = (bf16[2048,256]{1,0:T(8,128)(2,1)}, bf16[2048,256]{1,0:T(8,128)(2,1)S(1)}, u32[]{:S(2)}) copy-start(bf16[2048,256]{1,0:T(8,128)(2,1)S(1)} %pad_maximum_fusion.13.refs_0_) | copy-start | bytes 3145732
  413.5 26.3 %collective-permute-start.28 = (bf16[1152,128]{1,0:T(8,128)(2,1)S(1)}, bf16[1152,128]{1,0:T(8,128)(2,1)S(1)}, u32[]{:S(2)}, u32[]{:S(2)}) collective-permute-start(bf16[1152,128]{1,0:T(8,128)(2,1)S(1)} %slice.466), channel_id=1, source_target_pairs={{0,4},{2,6},{4,0},{6,2},{8,12},{10,14},{12,8},{14,10},{16,20},{18,... | collective-permute-start | bytes 884744 | tf_op jit(solution)/shard_map/ppermute | solution.py:589
  436.3 6.9 %collective-permute-start.39 = (bf16[1184,128]{1,0:T(8,128)(2,1)S(1)}, bf16[1184,128]{1,0:T(8,128)(2,1)S(1)}, u32[]{:S(2)}, u32[]{:S(2)}) collective-permute-start(bf16[1184,128]{1,0:T(8,128)(2,1)S(1)} %slice.465), channel_id=1, source_target_pairs={{0,1},{1,0},{2,3},{3,2},{4,5},{5,4},{6,7},{7,6},{8,9},{9,8},{10,11... | collective-permute-start | bytes 909320 | tf_op jit(solution)/shard_map/ppermute | solution.py:589
  440.0 6.6 %collective-permute-start.31 = (bf16[288,128]{1,0:T(8,128)(2,1)S(1)}, bf16[288,128]{1,0:T(8,128)(2,1)S(1)}, u32[]{:S(2)}, u32[]{:S(2)}) collective-permute-start(bf16[288,128]{1,0:T(8,128)(2,1)S(1)} %get-tuple-element.113), channel_id=1, source_target_pairs={{0,24},{2,26},{4,28},{6,30},{8,0},{10,2},{12,4},{14,6},{16,8},{18,... | collective-permute-start | bytes 221192 | tf_op jit(solution)/shard_map/ppermute | solution.py:653
  440.1 7.3 %collective-permute-start.30 = (bf16[288,128]{1,0:T(8,128)(2,1)S(1)}, bf16[288,128]{1,0:T(8,128)(2,1)S(1)}, u32[]{:S(2)}, u32[]{:S(2)}) collective-permute-start(bf16[288,128]{1,0:T(8,128)(2,1)S(1)} %get-tuple-element.114), channel_id=1, source_target_pairs={{0,16},{2,18},{4,20},{6,22},{8,24},{10,26},{12,28},{14,30},{16,0},... | collective-permute-start | bytes 221192 | tf_op jit(solution)/shard_map/ppermute | solution.py:653
  443.2 6.7 %collective-permute-start.29 = (bf16[288,128]{1,0:T(8,128)(2,1)S(1)}, bf16[288,128]{1,0:T(8,128)(2,1)S(1)}, u32[]{:S(2)}, u32[]{:S(2)}) collective-permute-start(bf16[288,128]{1,0:T(8,128)(2,1)S(1)} %get-tuple-element.112), channel_id=1, source_target_pairs={{0,8},{2,10},{4,12},{6,14},{8,16},{10,18},{12,20},{14,22},{16,24},... | collective-permute-start | bytes 221192 | tf_op jit(solution)/shard_map/ppermute | solution.py:653
  446.5 5.5 %collective-permute-start.42 = (bf16[296,128]{1,0:T(8,128)(2,1)S(1)}, bf16[296,128]{1,0:T(8,128)(2,1)S(1)}, u32[]{:S(2)}, u32[]{:S(2)}) collective-permute-start(bf16[296,128]{1,0:T(8,128)(2,1)S(1)} %get-tuple-element.110), channel_id=1, source_target_pairs={{0,24},{2,26},{4,28},{6,30},{8,0},{10,2},{12,4},{14,6},{16,8},{18,... | collective-permute-start | bytes 227336 | tf_op jit(solution)/shard_map/ppermute | solution.py:653
  447.4 9.1 %collective-permute-start.41 = (bf16[296,128]{1,0:T(8,128)(2,1)S(1)}, bf16[296,128]{1,0:T(8,128)(2,1)S(1)}, u32[]{:S(2)}, u32[]{:S(2)}) collective-permute-start(bf16[296,128]{1,0:T(8,128)(2,1)S(1)} %get-tuple-element.111), channel_id=1, source_target_pairs={{0,16},{2,18},{4,20},{6,22},{8,24},{10,26},{12,28},{14,30},{16,0},... | collective-permute-start | bytes 227336 | tf_op jit(solution)/shard_map/ppermute | solution.py:653
  449.9 7.0 %collective-permute-start.40 = (bf16[296,128]{1,0:T(8,128)(2,1)S(1)}, bf16[296,128]{1,0:T(8,128)(2,1)S(1)}, u32[]{:S(2)}, u32[]{:S(2)}) collective-permute-start(bf16[296,128]{1,0:T(8,128)(2,1)S(1)} %get-tuple-element.109), channel_id=1, source_target_pairs={{0,8},{2,10},{4,12},{6,14},{8,16},{10,18},{12,20},{14,22},{16,24},... | collective-permute-start | bytes 227336 | tf_op jit(solution)/shard_map/ppermute | solution.py:653
  452.0 6.8 %collective-permute-start.34 = (bf16[288,128]{1,0:T(8,128)(2,1)S(1)}, bf16[288,128]{1,0:T(8,128)(2,1)S(1)}, u32[]{:S(2)}, u32[]{:S(2)}) collective-permute-start(bf16[288,128]{1,0:T(8,128)(2,1)S(1)} %add_convert_fusion.3), channel_id=1, source_target_pairs={{0,24},{2,26},{4,28},{6,30},{8,0},{10,2},{12,4},{14,6},{16,8},{18,... | collective-permute-start | bytes 221192 | tf_op jit(solution)/shard_map/ppermute | solution.py:653
  456.5 5.7 %collective-permute-start.33 = (bf16[288,128]{1,0:T(8,128)(2,1)S(1)}, bf16[288,128]{1,0:T(8,128)(2,1)S(1)}, u32[]{:S(2)}, u32[]{:S(2)}) collective-permute-start(bf16[288,128]{1,0:T(8,128)(2,1)S(1)} %add_convert_fusion.3), channel_id=1, source_target_pairs={{0,16},{2,18},{4,20},{6,22},{8,24},{10,26},{12,28},{14,30},{16,0},... | collective-permute-start | bytes 221192 | tf_op jit(solution)/shard_map/ppermute | solution.py:653
  456.8 6.2 %collective-permute-start.32 = (bf16[288,128]{1,0:T(8,128)(2,1)S(1)}, bf16[288,128]{1,0:T(8,128)(2,1)S(1)}, u32[]{:S(2)}, u32[]{:S(2)}) collective-permute-start(bf16[288,128]{1,0:T(8,128)(2,1)S(1)} %add_convert_fusion.3), channel_id=1, source_target_pairs={{0,8},{2,10},{4,12},{6,14},{8,16},{10,18},{12,20},{14,22},{16,24},... | collective-permute-start | bytes 221192 | tf_op jit(solution)/shard_map/ppermute | solution.py:653
  458.9 5.8 %collective-permute-start.45 = (bf16[296,128]{1,0:T(8,128)(2,1)S(1)}, bf16[296,128]{1,0:T(8,128)(2,1)S(1)}, u32[]{:S(2)}, u32[]{:S(2)}) collective-permute-start(bf16[296,128]{1,0:T(8,128)(2,1)S(1)} %add_convert_fusion.2), channel_id=1, source_target_pairs={{0,24},{2,26},{4,28},{6,30},{8,0},{10,2},{12,4},{14,6},{16,8},{18,... | collective-permute-start | bytes 227336 | tf_op jit(solution)/shard_map/ppermute | solution.py:653
  462.3 5.3 %collective-permute-start.44 = (bf16[296,128]{1,0:T(8,128)(2,1)S(1)}, bf16[296,128]{1,0:T(8,128)(2,1)S(1)}, u32[]{:S(2)}, u32[]{:S(2)}) collective-permute-start(bf16[296,128]{1,0:T(8,128)(2,1)S(1)} %add_convert_fusion.2), channel_id=1, source_target_pairs={{0,16},{2,18},{4,20},{6,22},{8,24},{10,26},{12,28},{14,30},{16,0},... | collective-permute-start | bytes 227336 | tf_op jit(solution)/shard_map/ppermute | solution.py:653
  463.1 6.2 %collective-permute-start.43 = (bf16[296,128]{1,0:T(8,128)(2,1)S(1)}, bf16[296,128]{1,0:T(8,128)(2,1)S(1)}, u32[]{:S(2)}, u32[]{:S(2)}) collective-permute-start(bf16[296,128]{1,0:T(8,128)(2,1)S(1)} %add_convert_fusion.2), channel_id=1, source_target_pairs={{0,8},{2,10},{4,12},{6,14},{8,16},{10,18},{12,20},{14,22},{16,24},... | collective-permute-start | bytes 227336 | tf_op jit(solution)/shard_map/ppermute | solution.py:653
  464.7 27.6 %collective-permute-start.25 = (bf16[2048,256]{1,0:T(8,128)(2,1)S(1)}, bf16[2048,256]{1,0:T(8,128)(2,1)}, u32[]{:S(2)}, u32[]{:S(2)}) collective-permute-start(bf16[2048,256]{1,0:T(8,128)(2,1)S(1)} %pad_maximum_fusion.13.refs_0_), channel_id=1, source_target_pairs={{0,2},{2,0},{4,6},{6,4},{8,10},{10,8},{12,14},{14,12},{16,18},{18,... | collective-permute-start | bytes 3145736 | tf_op jit(solution)/shard_map/ppermute | solution.py:589
  467.6 9.9 %collective-permute-start.35 = (bf16[1152,128]{1,0:T(8,128)(2,1)S(1)}, bf16[1152,128]{1,0:T(8,128)(2,1)S(1)}, u32[]{:S(2)}, u32[]{:S(2)}) collective-permute-start(bf16[1152,128]{1,0:T(8,128)(2,1)S(1)} %pad_maximum_fusion.35), channel_id=1, source_target_pairs={{0,4},{2,6},{4,0},{6,2},{8,12},{10,14},{12,8},{14,10},{16,20},{18,... | collective-permute-start | bytes 884744 | tf_op jit(solution)/shard_map/ppermute | solution.py:589
  469.3 11.4 %collective-permute-start.46 = (bf16[1184,128]{1,0:T(8,128)(2,1)S(1)}, bf16[1184,128]{1,0:T(8,128)(2,1)S(1)}, u32[]{:S(2)}, u32[]{:S(2)}) collective-permute-start(bf16[1184,128]{1,0:T(8,128)(2,1)S(1)} %pad_maximum_fusion.34), channel_id=1, source_target_pairs={{0,4},{2,6},{4,0},{6,2},{8,12},{10,14},{12,8},{14,10},{16,20},{18,... | collective-permute-start | bytes 909320 | tf_op jit(solution)/shard_map/ppermute | solution.py:589
  470.0 18.5 %collective-permute-start.56 = (bf16[1024,512]{1,0:T(8,128)(2,1)S(1)}, bf16[1024,512]{1,0:T(8,128)(2,1)}, u32[]{:S(2)}, u32[]{:S(2)}) collective-permute-start(bf16[1024,512]{1,0:T(8,128)(2,1)S(1)} %pad_maximum_fusion.14.refs_0_), channel_id=1, source_target_pairs={{0,2},{2,0},{4,6},{6,4},{8,10},{10,8},{12,14},{14,12},{16,18},{18,... | collective-permute-start | bytes 3145736 | tf_op jit(solution)/shard_map/ppermute | solution.py:589
  478.4 14.0 %collective-permute-start.36 = (bf16[1152,256]{1,0:T(8,128)(2,1)}, bf16[1152,256]{1,0:T(8,128)(2,1)}, u32[]{:S(2)}, u32[]{:S(2)}) collective-permute-start(bf16[1152,256]{1,0:T(8,128)(2,1)} %pad_maximum_fusion.21.refs_2_), channel_id=1, source_target_pairs={{0,2},{2,0},{4,6},{6,4},{8,10},{10,8},{12,14},{14,12},{16,18},{18,... | collective-permute-start | bytes 1769480 | tf_op jit(solution)/shard_map/ppermute | solution.py:589
  480.8 11.5 %collective-permute-start.47 = (bf16[1184,256]{1,0:T(8,128)(2,1)S(1)}, bf16[1184,256]{1,0:T(8,128)(2,1)}, u32[]{:S(2)}, u32[]{:S(2)}) collective-permute-start(bf16[1184,256]{1,0:T(8,128)(2,1)S(1)} %pad_maximum_fusion.20.refs_4_), channel_id=1, source_target_pairs={{0,2},{2,0},{4,6},{6,4},{8,10},{10,8},{12,14},{14,12},{16,18},{18,... | collective-permute-start | bytes 1818632 | tf_op jit(solution)/shard_map/ppermute | solution.py:589
  480.9 4.5 collective-permute-start.16
  (67 other events, 483.4 us)
